TPU v7x, 32 devices: a whole 2x2x4 slice. The times are simulated.
32 devices in a mesh: img: 4 (over y, core), gz: 8 (over z, x).
Axes of the slice: x: 2, y: 2, z: 4, core: 2. Of those that a mesh axis runs over, the one named last changes fastest.
Arguments:
- images: float32 [16, 5, 16, 128, 128], P('img', None, 'gz'), may hold values from -12 to 12
- centre: int32 [16], P('img'), may hold values from 1 to 14, as said below
- positions: float32 [16], P('img'), may hold values from 0 to 1
Outputs:
- path: float32 [16, 5, 16, 128, 128], P('img', None, 'gz')
Inputs may be any that keep to these rules, and one draw needn't show every extreme that they name: `centre`: centre_m lies within m - 1 to m + 1, clipped to 1 to 14; at the first target of each aligned block of 4 it is m - 1 and at the last m + 1, before clipping.
All inputs are finite; a program needn't handle non-finite values.
Results may differ from a plain program's by a relative error of at most 0.0003.
Values sent between devices are 32-bit elements; how exact they have to be, the bound alone decides.
A program may use at most 64 MiB of HBM per device.

v0:
```python
import math

import jax
import jax.numpy as jnp
from jax import lax
from jax.sharding import PartitionSpec as P

elastic = 1.0
chiral_weight = 0.5
bulk_linear = -0.2
bulk_cubic = 0.5
bulk_quartic = 0.1
step_size = 1.0
smoothing = 64.0
epsilon = 1e-06
slot_pairs = ((0, 0), (0, 1), (0, 2), (1, 1), (1, 2))
slot_index = {(0, 0): 0, (0, 1): 1, (0, 2): 2, (1, 1): 3, (1, 2): 4}
pattern_x = "kx,abzxy->abzky"
pattern_y = "ky,abzxy->abzxk"
pattern_z = "kz,abzxy->abkxy"


def padded_2(block, sides, width, periodic):
    for axis, dim in sides:
        count = lax.axis_size(axis)
        forward = [(i, i + 1) for i in range(count - 1)]
        if periodic:
            forward.append((count - 1, 0))
        backward = [(target, source) for source, target in forward]
        low = lax.ppermute(
            lax.slice_in_dim(block, block.shape[dim] - width, None, axis=dim), axis, forward
        )
        high = lax.ppermute(lax.slice_in_dim(block, 0, width, axis=dim), axis, backward)
        block = jnp.concatenate([low, block, high], axis=dim)
    return block


def levi(first, middle, last):
    return (first - middle) * (middle - last) * (last - first) // 2


def tensor_entry(fields, row, column):
    if row > column:
        row, column = (column, row)
    if row == 2:
        return -(fields[0] + fields[3])
    return fields[slot_index[row, column]]


def nonlinear_drive(padded):
    fields_pad = [padded[:, slot] for slot in range(5)]
    centre_fields = [field[:, 1:-1] for field in fields_pad]
    grad_x = [(jnp.roll(field, -1, 2) - jnp.roll(field, 1, 2)) * 0.5 for field in centre_fields]
    grad_y = [(jnp.roll(field, -1, 3) - jnp.roll(field, 1, 3)) * 0.5 for field in centre_fields]
    grad_z = [(field[:, 2:] - field[:, :-2]) * 0.5 for field in fields_pad]
    gradients = (grad_x, grad_y, grad_z)
    laplace = []
    for field, inner in zip(fields_pad, centre_fields):
        value = field[:, 2:] + field[:, :-2] + jnp.roll(inner, 1, 2) + jnp.roll(inner, -1, 2)
        value = value + jnp.roll(inner, 1, 3) + jnp.roll(inner, -1, 3) - 6.0 * inner
        laplace.append(value)

    def curl_entry(row, column):
        total = jnp.zeros_like(centre_fields[0])
        for middle in range(3):
            for last in range(3):
                sign = levi(row, middle, last)
                if sign != 0:
                    total = total + sign * tensor_entry(gradients[middle], last, column)
        return total

    def square_entry(row, column):
        total = jnp.zeros_like(centre_fields[0])
        for middle in range(3):
            total = total + tensor_entry(centre_fields, row, middle) * tensor_entry(
                centre_fields, middle, column
            )
        return total

    trace = square_entry(0, 0) + square_entry(1, 1) + square_entry(2, 2)
    results = []
    for slot, pair in enumerate(slot_pairs):
        row, column = pair
        value = centre_fields[slot]
        chiral = curl_entry(row, column) + curl_entry(column, row)
        square = square_entry(row, column)
        if row == column:
            square = square - trace / 3.0
        bulk = bulk_linear * value - bulk_cubic * square + bulk_quartic * trace * value
        results.append(elastic * laplace[slot] - chiral_weight * chiral - bulk)
    return jnp.stack(results, axis=1)


def symbol_line(wave, length):
    return 2.0 - 2.0 * jnp.cos(2.0 * math.pi / length * wave.astype(jnp.float32))


def dft_tables(length):
    index = jnp.arange(length, dtype=jnp.int32)
    angle = 2.0 * math.pi / length * (index[:, None] * index[None, :] % length).astype(jnp.float32)
    return (jnp.cos(angle), jnp.sin(angle))


def apply_table(table, field, pattern):
    return jnp.einsum(pattern, table, field, precision=lax.Precision.HIGHEST)


def interp_matrix(arc, centre, target, columns, offset):
    nodes_index = jnp.arange(arc.shape[0], dtype=jnp.int32)

    def pick(where_at):
        return jnp.sum(
            arc[None, :] * (nodes_index[None, :] == where_at[:, None]).astype(jnp.float32), axis=1
        )

    before = pick(centre - 1)
    middle = pick(centre)
    after = pick(centre + 1)
    weight_before = (target - middle) * (target - after) / ((before - middle) * (before - after))
    weight_middle = (target - before) * (target - after) / ((middle - before) * (middle - after))
    weight_after = (target - before) * (target - middle) / ((after - before) * (after - middle))
    column_index = jnp.arange(columns, dtype=jnp.int32)
    matrix = jnp.zeros((centre.shape[0], columns), jnp.float32)
    for shift_by, weight in ((-1, weight_before), (0, weight_middle), (1, weight_after)):
        spot = centre + shift_by - offset
        matrix = matrix + weight[:, None] * (column_index[None, :] == spot[:, None]).astype(
            jnp.float32
        )
    return matrix


def local(images, centre, positions):
    count_img = images.shape[0]
    slab = images.shape[2]
    width_x = images.shape[3]
    width_y = images.shape[4]
    groups = lax.axis_size("gz")
    depth = slab * groups
    block = width_x // groups
    padded = padded_2(images, (("gz", 2),), 1, True)
    drive = nonlinear_drive(padded)
    wave_x = lax.axis_index("gz") * block + jnp.arange(block, dtype=jnp.int32)
    symbol = symbol_line(jnp.arange(depth, dtype=jnp.int32), depth)[:, None, None]
    symbol = symbol + symbol_line(wave_x, width_x)[None, :, None]
    symbol = symbol + symbol_line(jnp.arange(width_y, dtype=jnp.int32), width_y)[None, None, :]
    multiplier = step_size / ((1.0 + smoothing * symbol) * float(width_x * width_y * depth))
    cos_x, sin_x = dft_tables(width_x)
    cos_y, sin_y = dft_tables(width_y)
    cos_z, sin_z = dft_tables(depth)
    cas_x = cos_x + sin_x
    cas_y = cos_y + sin_y
    cas_z = cos_z + sin_z
    spread = apply_table(cas_y, apply_table(cas_x, drive, pattern_x), pattern_y)
    spectrum = (
        apply_table(
            cas_z, lax.all_to_all(spread, "gz", split_axis=3, concat_axis=2, tiled=True), pattern_z
        )
        * multiplier
    )
    gathered = lax.all_to_all(
        apply_table(cas_z, spectrum, pattern_z), "gz", split_axis=2, concat_axis=3, tiled=True
    )
    update = apply_table(cas_x, apply_table(cas_y, gathered, pattern_y), pattern_x)
    stepped = images + update
    extended = padded_2(stepped, (("img", 0),), 2, False)
    gaps = extended[3 : count_img + 3] - extended[2 : count_img + 2]
    pair_sums = jnp.sum(gaps * gaps, axis=(1, 2, 3, 4))
    total_images = count_img * lax.axis_size("img")
    first_image = lax.axis_index("img") * count_img
    slab_sums = lax.psum(pair_sums, "gz")
    totals = lax.all_gather(slab_sums, "img", axis=0, tiled=True)
    cells = 5.0 * depth * width_x * width_y
    global_index = jnp.arange(total_images, dtype=jnp.int32)
    dist = jnp.where(global_index < total_images - 1, jnp.sqrt(totals / cells + epsilon), 0.0)
    arc = jnp.cumsum(dist) - dist
    target = positions * arc[-1]
    matrix = interp_matrix(arc, centre, target, count_img + 4, first_image - 2)
    return jnp.einsum("mr,rqzxy->mqzxy", matrix, extended, precision=lax.Precision.HIGHEST)


def solution(mesh):
    in_specs = (P("img", None, "gz", None, None), P("img"), P("img"))
    out_specs = P("img", None, "gz", None, None)
    return jax.shard_map(local, mesh=mesh, in_specs=in_specs, out_specs=out_specs, check_vma=False)
```

profile of v0, /device:TPU:1, one launch (start us, length us, event | category | flops | bytes accessed | tf_op | source)
XLA Modules:
  0.0 305.3 jit_solution(2030836855031090911)
XLA Ops:
  0.0 2.1 copy.58
  2.3 2.1 collective-permute-start
  4.4 3.1 %collective-permute-start.1 = (f32[4,5,1,128,128]{3,4,2,0,1:T(8,128)S(1)}, f32[4,5,1,128,128]{3,4,2,0,1:T(8,128)S(1)}, u32[]{:S(2)}, u32[]{:S(2)}) collective-permute-start(f32[4,5,1,128,128]{3,4,2,0,1:T(8,128)S(1)} %get-tuple-element.19), channel_id=1, source_target_pairs={{1,0},{2,1},{3,2},{4,3},{5,4},{6,5},{7,6},{0,7},{9,8},{10,9},{11,1... | collective-permute-start | bytes 3932168 | tf_op jit(solution)/shard_map/ppermute | solution.py:33
  7.5 52.4 %collective-permute-done = f32[4,5,1,128,128]{3,4,2,0,1:T(8,128)S(1)} collective-permute-done((f32[4,5,1,128,128]{3,4,2,0,1:T(8,128)S(1)}, f32[4,5,1,128,128]{3,4,2,0,1:T(8,128)S(1)}, u32[]{:S(2)}, u32[]{:S(2)}) %collective-permute-start) | collective-permute-done | bytes 1310752 | tf_op jit(solution)/shard_map/ppermute | solution.py:30
  71.0 2.6 fusion.21
  73.6 14.2 %fusion.4 = f32[4,5,2,128,128]{4,3,2,1,0:T(8,128)S(1)} fusion(f32[4,5,2,128,128]{4,3,2,1,0:T(8,128)S(1)} %fusion.21), kind=kOutput, calls=%fused_computation.9 | convolution fusion | flops 1006878720 | bytes 5242880 | tf_op jit(solution)/shard_map/ky,abzxy->abzxk/dot_general | solution.py:105
  87.7 3.5 %copy.66 = f32[4,5,2,128,128]{4,2,1,0,3:T(2,128)} copy(f32[4,5,2,128,128]{4,3,2,1,0:T(8,128)S(1)} %fusion.4) | data formatting | bytes 5242880 | tf_op jit(solution)/shard_map/ky,abzxy->abzxk/dot_general | solution.py:105
  91.3 5.7 %all-to-all-start = ((f32[4,5,2,128,128]{4,2,1,0,3:T(2,128)}), f32[4,5,2,128,128]{4,2,1,0,3:T(2,128)S(1)}, u32[]{:S(2)}, u32[]{:S(2)}) async-start(f32[4,5,2,128,128]{4,2,1,0,3:T(2,128)} %copy.66), calls=%async_computation | async-start | bytes 5242880 | tf_op jit(solution)/shard_map/all_to_all | solution.py:156
  97.2 58.5 %all-to-all-done = f32[4,5,2,128,128]{4,2,1,0,3:T(2,128)S(1)} async-done(((f32[4,5,2,128,128]{4,2,1,0,3:T(2,128)}), f32[4,5,2,128,128]{4,2,1,0,3:T(2,128)S(1)}, u32[]{:S(2)}, u32[]{:S(2)}) %all-to-all-start) | async-done | bytes 2621472 | tf_op jit(solution)/shard_map/all_to_all | solution.py:156
  156.6 3.1 fusion.6
  159.6 2.6 fusion.8
  162.2 2.3 copy.70
  164.5 4.8 %all-to-all-start.1 = ((f32[4,5,16,16,128]{4,3,1,0,2:T(8,128)}), f32[4,5,16,16,128]{4,3,1,0,2:T(8,128)}, u32[]{:S(2)}, u32[]{:S(2)}) async-start(f32[4,5,16,16,128]{4,3,1,0,2:T(8,128)} %copy.70), calls=%async_computation.1 | async-start | bytes 5242880 | tf_op jit(solution)/shard_map/all_to_all | solution.py:160
  171.4 56.2 %all-to-all-done.1 = f32[4,5,16,16,128]{4,3,1,0,2:T(8,128)} async-done(((f32[4,5,16,16,128]{4,3,1,0,2:T(8,128)}), f32[4,5,16,16,128]{4,3,1,0,2:T(8,128)}, u32[]{:S(2)}, u32[]{:S(2)}) %all-to-all-start.1) | async-done | bytes 2621472 | tf_op jit(solution)/shard_map/all_to_all | solution.py:160
  229.7 2.8 fusion.18
  232.5 2.6 bitcast_add_fusion
  236.8 4.2 %collective-permute-start.2 = (f32[2,5,2,128,128]{3,4,2,1,0:T(8,128)}, f32[2,5,2,128,128]{3,4,2,1,0:T(8,128)}, u32[]{:S(2)}, u32[]{:S(2)}) collective-permute-start(f32[2,5,2,128,128]{3,4,2,1,0:T(8,128)} %get-tuple-element.17), channel_id=1, source_target_pairs={{8,0},{16,8},{24,16},{9,1},{17,9},{25,17},{10,2},{18,10},{26,18},{... | collective-permute-start | bytes 3932168 | tf_op jit(solution)/shard_map/ppermute | solution.py:33
  241.0 3.1 %collective-permute-start.3 = (f32[2,5,2,128,128]{3,4,2,1,0:T(8,128)}, f32[2,5,2,128,128]{3,4,2,1,0:T(8,128)}, u32[]{:S(2)}, u32[]{:S(2)}) collective-permute-start(f32[2,5,2,128,128]{3,4,2,1,0:T(8,128)} %get-tuple-element.16), channel_id=1, source_target_pairs={{0,8},{8,16},{16,24},{1,9},{9,17},{17,25},{2,10},{10,18},{18,26},{... | collective-permute-start | bytes 3932168 | tf_op jit(solution)/shard_map/ppermute | solution.py:30
  244.7 13.2 %collective-permute-done.2 = f32[2,5,2,128,128]{3,4,2,1,0:T(8,128)} collective-permute-done((f32[2,5,2,128,128]{3,4,2,1,0:T(8,128)}, f32[2,5,2,128,128]{3,4,2,1,0:T(8,128)}, u32[]{:S(2)}, u32[]{:S(2)}) %collective-permute-start.2) | collective-permute-done | bytes 1310752 | tf_op jit(solution)/shard_map/ppermute | solution.py:33
  260.1 15.7 %psum.7 = f32[4]{0:T(128)S(1)} all-reduce(f32[4]{0:T(128)S(1)} %fusion.2), channel_id=1, replica_groups=mesh['img'=4,'gz'=8] {'gz'}, use_global_device_ids=true, to_apply=%region_1.2 | all-reduce | flops 4 | bytes 32 | tf_op jit(solution)/shard_map/psum | solution.py:170
  276.1 7.4 %all-reduce = f32[16]{0:T(128)S(1)} all-reduce(f32[16]{0:T(128)S(1)} %dynamic-update-slice), channel_id=1, replica_groups=mesh['img'=4,'gz'=8] {'img'}, use_global_device_ids=true, to_apply=%add | all-reduce | flops 16 | bytes 128
  284.3 4.5 %pad_maximum_fusion.1 = f32[8,5,2,128,128]{3,4,2,1,0:T(8,128)} fusion(f32[2,5,2,128,128]{3,4,2,1,0:T(8,128)} %collective-permute-done.2, f32[4,5,2,128,128]{3,4,2,1,0:T(8,128)S(1)} %bitcast_add_fusion, f32[2,5,2,128,128]{3,4,2,1,0:T(8,128)} %collective-permute-done.3), kind=kLoop, calls=%fused_computation.1 | loop fusion | flops 2621440 | bytes 10485760 | tf_op jit(solution)/shard_map/concatenate | solution.py:34
  288.8 6.1 %copy.76 = f32[8,5,2,128,128]{4,0,3,2,1:T(8,128)} copy(f32[8,5,2,128,128]{3,4,2,1,0:T(8,128)} %pad_maximum_fusion.1) | data formatting | bytes 10485760 | tf_op jit(solution)/shard_map/concatenate | solution.py:34
  295.8 7.3 %fusion.34 = f32[4,5,2,128,128]{4,0,3,2,1:T(4,128)S(1)} fusion(f32[8,5,2,128,128]{4,0,3,2,1:T(8,128)} %copy.76, f32[4]{0:T(128)S(1)} %get-tuple-element.62, s32[4]{0:T(128)S(1)} %get-tuple-element.67, f32[4]{0:T(128)S(1)} %get-tuple-element.61, s32[4]{0:T(128)S(1)} %get-tuple-element.66, f32[4]{0:T(128)S(1)} %get-tuple-element.60, s32[4]{0:T(128)S(1)} %get-tuple-element.63), kind=kOutput, calls=%fused_computation.85 | convolution fusion | flops 62914816 | bytes 7864416 | tf_op jit(solution)/shard_map/mr,rqzxy->mqzxy/dot_general | solution.py:178
  (55 shorter events, 24.0 us)
Async XLA Ops:
  2.3 57.6 %collective-permute-start = (f32[4,5,1,128,128]{3,4,2,0,1:T(8,128)S(1)}, f32[4,5,1,128,128]{3,4,2,0,1:T(8,128)S(1)}, u32[]{:S(2)}, u32[]{:S(2)}) collective-permute-start(f32[4,5,1,128,128]{3,4,2,0,1:T(8,128)S(1)} %get-tuple-element.18), channel_id=1, source_target_pairs={{0,1},{1,2},{2,3},{3,4},{4,5},{5,6},{6,7},{7,0},{8,9},{9,10},{10,1... | collective-permute-start | bytes 3932168 | tf_op jit(solution)/shard_map/ppermute | solution.py:30
  4.4 57.4 %collective-permute-start.1 = (f32[4,5,1,128,128]{3,4,2,0,1:T(8,128)S(1)}, f32[4,5,1,128,128]{3,4,2,0,1:T(8,128)S(1)}, u32[]{:S(2)}, u32[]{:S(2)}) collective-permute-start(f32[4,5,1,128,128]{3,4,2,0,1:T(8,128)S(1)} %get-tuple-element.19), channel_id=1, source_target_pairs={{1,0},{2,1},{3,2},{4,3},{5,4},{6,5},{7,6},{0,7},{9,8},{10,9},{11,1... | collective-permute-start | bytes 3932168 | tf_op jit(solution)/shard_map/ppermute | solution.py:33
  91.3 64.4 %all-to-all-start = ((f32[4,5,2,128,128]{4,2,1,0,3:T(2,128)}), f32[4,5,2,128,128]{4,2,1,0,3:T(2,128)S(1)}, u32[]{:S(2)}, u32[]{:S(2)}) async-start(f32[4,5,2,128,128]{4,2,1,0,3:T(2,128)} %copy.66), calls=%async_computation | async-start | bytes 5242880 | tf_op jit(solution)/shard_map/all_to_all | solution.py:156
  164.5 4.8 %copy-start = (f32[4,5,2,128,128]{4,3,2,1,0:T(8,128)S(1)}, f32[4,5,2,128,128]{4,3,2,1,0:T(8,128)}, u32[]{:S(2)}) copy-start(f32[4,5,2,128,128]{4,3,2,1,0:T(8,128)} %param.3) | copy-start | bytes 7864324
  164.5 63.1 %all-to-all-start.1 = ((f32[4,5,16,16,128]{4,3,1,0,2:T(8,128)}), f32[4,5,16,16,128]{4,3,1,0,2:T(8,128)}, u32[]{:S(2)}, u32[]{:S(2)}) async-start(f32[4,5,16,16,128]{4,3,1,0,2:T(8,128)} %copy.70), calls=%async_computation.1 | async-start | bytes 5242880 | tf_op jit(solution)/shard_map/all_to_all | solution.py:160
  229.7 2.8 copy-start.1
  235.1 9.0 %copy-start.4 = (u32[32]{0:T(128)S(1)}, u32[32]{0:T(128)}, u32[]{:S(2)}) copy-start(u32[32]{0:T(128)} %constant.107) | copy-start | bytes 388
  235.1 9.6 %copy-start.2 = (s32[4]{0:T(128)S(1)}, s32[4]{0:T(128)}, u32[]{:S(2)}) copy-start(s32[4]{0:T(128)} %param.4) | copy-start | bytes 52
  236.8 21.1 %collective-permute-start.2 = (f32[2,5,2,128,128]{3,4,2,1,0:T(8,128)}, f32[2,5,2,128,128]{3,4,2,1,0:T(8,128)}, u32[]{:S(2)}, u32[]{:S(2)}) collective-permute-start(f32[2,5,2,128,128]{3,4,2,1,0:T(8,128)} %get-tuple-element.17), channel_id=1, source_target_pairs={{8,0},{16,8},{24,16},{9,1},{17,9},{25,17},{10,2},{18,10},{26,18},{... | collective-permute-start | bytes 3932168 | tf_op jit(solution)/shard_map/ppermute | solution.py:33
  241.0 43.3 %collective-permute-start.3 = (f32[2,5,2,128,128]{3,4,2,1,0:T(8,128)}, f32[2,5,2,128,128]{3,4,2,1,0:T(8,128)}, u32[]{:S(2)}, u32[]{:S(2)}) collective-permute-start(f32[2,5,2,128,128]{3,4,2,1,0:T(8,128)} %get-tuple-element.16), channel_id=1, source_target_pairs={{0,8},{8,16},{16,24},{1,9},{9,17},{17,25},{2,10},{10,18},{18,26},{... | collective-permute-start | bytes 3932168 | tf_op jit(solution)/shard_map/ppermute | solution.py:30
  288.8 6.4 %copy-start.3 = (f32[4]{0:T(128)S(1)}, f32[4]{0:T(128)}, u32[]{:S(2)}) copy-start(f32[4]{0:T(128)} %param.5) | copy-start | bytes 52
where the time goes:
time: 310 us; the launch traced here: 305 us
  waiting for transfers between devices  182 us (59%)
  matrix products  35 us (11%)
  local copies, waits for them, and re-layouts  27.3 us (9%)
  blocking collectives  23.1 us (7%)
  starting transfers between devices  23 us (7%)
  other arithmetic  13.4 us (4%)
    all_to_all x1, waiting for transfers between devices, local(): lax.all_to_all(spread, 'gz', split_axis=3, concat_axis=2, tiled=True)  58.5 us
    all_to_all x1, waiting for transfers between devices, local(): lax.all_to_all(apply_table(cas_z, spectrum, pattern_z), 'gz', split_axis=...  56.2 us
    ppermute x2, waiting for transfers between devices, padded_2(): lax.ppermute(lax.slice_in_dim(block, block.shape[dim] - width, None, axis...  52.4 us
    dot_general x6, matrix products, apply_table(): return jnp.einsum(pattern, table, field, precision=lax.Precision.HIGHEST)  27.7 us
    psum x1, blocking collectives, local(): slab_sums = lax.psum(pair_sums, 'gz')  15.7 us
    ppermute x2, waiting for transfers between devices, padded_2(): lax.ppermute(lax.slice_in_dim(block, 0, width, axis=dim), axis, backward)  15.1 us
    unnamed x1, blocking collectives  7.41 us
    ppermute x2, starting transfers between devices, padded_2(): lax.ppermute(lax.slice_in_dim(block, 0, width, axis=dim), axis, backward)  7.31 us
  transfers between devices with their start and end apart: 6, of which 5 were waited for; matrix products, arithmetic and copies ran while one was open for 2% of the time, Pallas kernels for 0%

commit v1 on v0

v1 whole, which is shorter than its diff:
```python
import math

import jax
import jax.numpy as jnp
from jax import lax
from jax.sharding import PartitionSpec as P

elastic = 1.0
chiral_weight = 0.5
bulk_linear = -0.2
bulk_cubic = 0.5
bulk_quartic = 0.1
step_size = 1.0
smoothing = 64.0
epsilon = 1e-06
chunks = 2


def shift_along(block, axis, step, periodic):
    count = lax.axis_size(axis)
    pairs = [(i, i + step) for i in range(count) if 0 <= i + step < count]
    if periodic:
        pairs = [(i, (i + step) % count) for i in range(count)]
    return lax.ppermute(block, axis, pairs)


def z_sources(images):
    return jnp.stack(
        [images[:, 1], images[:, 2], images[:, 4], images[:, 0] - images[:, 3]], axis=1
    )


def local_drive(images, low, high):
    q1, q2, q3, q4, q5 = (images[:, slot] for slot in range(5))
    q6 = -(q1 + q4)

    def grad_x(field):
        return (jnp.roll(field, -1, 2) - jnp.roll(field, 1, 2)) * 0.5

    def grad_y(field):
        return (jnp.roll(field, -1, 3) - jnp.roll(field, 1, 3)) * 0.5

    def grad_z(field, slot):
        padded = jnp.concatenate([low[:, slot], field, high[:, slot]], axis=1)
        return (padded[:, 2:] - padded[:, :-2]) * 0.5

    z2 = grad_z(q2, 0)
    z3 = grad_z(q3, 1)
    z5 = grad_z(q5, 2)
    z14 = grad_z(q1 - q4, 3)
    chiral = (
        2.0 * (grad_y(q3) - z2),
        grad_y(q5) - grad_x(q3) + z14,
        grad_y(q6 - q1) + grad_x(q2) - z5,
        2.0 * (z2 - grad_x(q5)),
        z3 + grad_x(q4 - q6) - grad_y(q2),
    )
    s1 = q1 * q1 + q2 * q2 + q3 * q3
    s4 = q2 * q2 + q4 * q4 + q5 * q5
    trace = s1 + s4 + q3 * q3 + q5 * q5 + q6 * q6
    square = (
        s1 - trace / 3.0,
        q1 * q2 + q2 * q4 + q3 * q5,
        q1 * q3 + q2 * q5 + q3 * q6,
        s4 - trace / 3.0,
        q2 * q3 + q4 * q5 + q5 * q6,
    )
    results = []
    for value, curl, product in zip((q1, q2, q3, q4, q5), chiral, square):
        bulk = bulk_linear * value - bulk_cubic * product + bulk_quartic * trace * value
        results.append((elastic / smoothing) * value - chiral_weight * curl - bulk)
    return jnp.stack(results, axis=1)


def symbol_line(wave, length):
    return 2.0 - 2.0 * jnp.cos(2.0 * math.pi / length * wave.astype(jnp.float32))


def cas_table(length):
    index = jnp.arange(length, dtype=jnp.int32)
    angle = 2.0 * math.pi / length * (index[:, None] * index[None, :] % length).astype(jnp.float32)
    return jnp.cos(angle) + jnp.sin(angle)


def apply_table(table, field, pattern):
    return jnp.einsum(pattern, table, field, precision=lax.Precision.HIGH)


def interp_matrix(arc, centre, target, columns, offset):
    nodes_index = jnp.arange(arc.shape[0], dtype=jnp.int32)

    def pick(where_at):
        return jnp.sum(jnp.where(nodes_index[None, :] == where_at[:, None], arc[None, :], 0.0), axis=1)

    before = pick(centre - 1)
    middle = pick(centre)
    after = pick(centre + 1)
    weight_before = (target - middle) * (target - after) / ((before - middle) * (before - after))
    weight_middle = (target - before) * (target - after) / ((middle - before) * (middle - after))
    weight_after = (target - before) * (target - middle) / ((after - before) * (after - middle))
    column_index = jnp.arange(columns, dtype=jnp.int32)
    matrix = jnp.zeros((centre.shape[0], columns), jnp.float32)
    for shift_by, weight in ((-1, weight_before), (0, weight_middle), (1, weight_after)):
        spot = centre + shift_by - offset
        matrix = matrix + jnp.where(column_index[None, :] == spot[:, None], weight[:, None], 0.0)
    return matrix


def local(images, centre, positions):
    count_img, _, slab, width_x, width_y = images.shape
    groups = lax.axis_size("gz")
    depth = slab * groups
    block = width_x // groups
    parts = chunks if count_img % chunks == 0 else 1
    each = count_img // parts
    wave_x = lax.axis_index("gz") * block + jnp.arange(block, dtype=jnp.int32)
    symbol = symbol_line(jnp.arange(depth, dtype=jnp.int32), depth)[:, None, None]
    symbol = symbol + symbol_line(wave_x, width_x)[None, :, None]
    symbol = symbol + symbol_line(jnp.arange(width_y, dtype=jnp.int32), width_y)[None, None, :]
    multiplier = step_size / ((1.0 + smoothing * symbol) * float(width_x * width_y * depth))
    multiplier = multiplier[:, None, None]
    cas_x = cas_table(width_x).reshape(groups, block, width_x)
    cas_y = cas_table(width_y)
    cas_z = cas_table(depth).reshape(depth, groups, slab)

    pieces = [images[i * each : (i + 1) * each] for i in range(parts)]
    halos = []
    for piece in pieces:
        low = shift_along(z_sources(piece[:, :, slab - 1 :]), "gz", 1, True)
        high = shift_along(z_sources(piece[:, :, :1]), "gz", -1, True)
        halos.append((low, high))
    stepped = []
    for piece, (low, high) in zip(pieces, halos):
        drive = local_drive(piece, low, high)
        spread = apply_table(cas_y, drive, "ky,abzxy->abzxk")
        spread = apply_table(cas_x, spread, "gkx,abzxy->gabzky")
        lines = lax.all_to_all(spread, "gz", split_axis=0, concat_axis=0)
        spectrum = apply_table(cas_z, lines, "wgz,gabzky->wabky") * multiplier
        solved = apply_table(cas_z, spectrum, "wgz,wabky->gabzky")
        gathered = lax.all_to_all(solved, "gz", split_axis=0, concat_axis=0)
        update = apply_table(cas_x, gathered, "gkx,gabzky->abzxy")
        update = apply_table(cas_y, update, "ky,abzxk->abzxy")
        stepped.append((1.0 - step_size * elastic / smoothing) * piece + update)

    single = [part[i : i + 1] for part in stepped for i in range(each)]
    reach = 2
    right = [shift_along(single[i], "img", -1, False) for i in range(reach)]
    left = [shift_along(single[count_img - reach + i], "img", 1, False) for i in range(reach)]
    extended = left + single + right

    total_images = count_img * lax.axis_size("img")
    first_image = lax.axis_index("img") * count_img
    pair_sums = []
    for i in range(count_img):
        gap = extended[reach + i + 1] - extended[reach + i]
        pair_sums.append(jnp.sum(gap * gap))
    sums = jnp.stack(pair_sums)
    global_index = jnp.arange(total_images, dtype=jnp.int32)
    own = global_index // count_img == lax.axis_index("img")
    totals = lax.psum(jnp.where(own, jnp.tile(sums, lax.axis_size("img")), 0.0), ("img", "gz"))
    cells = 5.0 * depth * width_x * width_y
    dist = jnp.where(global_index < total_images - 1, jnp.sqrt(totals / cells + epsilon), 0.0)
    earlier = global_index[None, :] < global_index[:, None]
    arc = jnp.sum(jnp.where(earlier, dist[None, :], 0.0), axis=1)
    target = positions * jnp.sum(dist)
    matrix = interp_matrix(arc, centre, target, count_img + 2 * reach, first_image - reach)
    path = []
    for m in range(count_img):
        terms = [matrix[m, m + d] * extended[m + d] for d in range(2 * reach + 1)]
        path.append(sum(terms[1:], terms[0]))
    return jnp.concatenate(path, axis=0)


def solution(mesh):
    in_specs = (P("img", None, "gz", None, None), P("img"), P("img"))
    out_specs = P("img", None, "gz", None, None)
    return jax.shard_map(local, mesh=mesh, in_specs=in_specs, out_specs=out_specs, check_vma=False)
```

time: 310 us -> 275 us (0.89); the launches traced: 305 us -> 274 us
  waiting for transfers between devices: 182 us -> 118 us
  starting transfers between devices: 23 us -> 44.7 us
  other arithmetic: 13.4 us -> 30.9 us
  blocking collectives: 23.1 us -> 40 us
  matrix products: 35 us -> 21.1 us
  local copies, waits for them, and re-layouts: 27.3 us -> 18.9 us
    ppermute x4 -> x8, waiting for transfers between devices: 67.5 us -> 29.5 us  [shift_along(): return lax.ppermute(block, axis, pairs)]
    all_to_all x2 -> x4, waiting for transfers between devices: 115 us -> 88.7 us  [the longest x2 45.5 us: local(): gathered = lax.all_to_all(solved, 'gz', split_axis=0, concat_axis=0)]
    psum x1, blocking collectives: 15.7 us -> 40 us  [local(): lax.psum(jnp.where(own, jnp.tile(sums, lax.axis_size('img')), 0.0), ('img...]
    add x0 -> x3, other arithmetic: none -> 16 us  [the longest x2 16 us: local(): path.append(sum(terms[1:], terms[0]))]
    dot_general x7 -> x12, matrix products: 35 us -> 21.1 us  [apply_table(): return jnp.einsum(pattern, table, field, precision=lax.Precision.HIGH)]
    ppermute x4 -> x8, starting transfers between devices: 12.5 us -> 23.7 us  [shift_along(): return lax.ppermute(block, axis, pairs)]
    all_to_all x2 -> x4, starting transfers between devices: 10.5 us -> 21 us  [the longest x2 10.8 us: local(): gathered = lax.all_to_all(solved, 'gz', split_axis=0, concat_axis=0)]
    unnamed x1 -> x0, blocking collectives: 7.41 us -> none
  transfers between devices with their start and end apart: 6 -> 12, of which waited for: 5 -> 7; matrix products, arithmetic and copies ran while one was open for 2% -> 19% of each run, Pallas kernels for 0% -> 0%
where the time goes in v1:
time: 275 us; the launch traced here: 274 us
  waiting for transfers between devices  118 us (43%)
  starting transfers between devices  44.7 us (16%)
  blocking collectives  40 us (15%)
  other arithmetic  30.9 us (11%)
  matrix products  21.1 us (8%)
  local copies, waits for them, and re-layouts  18.9 us (7%)
    all_to_all x2, waiting for transfers between devices, local(): gathered = lax.all_to_all(solved, 'gz', split_axis=0, concat_axis=0)  45.5 us
    all_to_all x2, waiting for transfers between devices, local(): lines = lax.all_to_all(spread, 'gz', split_axis=0, concat_axis=0)  43.2 us
    psum x1, blocking collectives, local(): lax.psum(jnp.where(own, jnp.tile(sums, lax.axis_size('img')), 0.0), ('img...  40 us
    ppermute x8, waiting for transfers between devices, shift_along(): return lax.ppermute(block, axis, pairs)  29.5 us
    ppermute x8, starting transfers between devices, shift_along(): return lax.ppermute(block, axis, pairs)  23.7 us
    dot_general x12, matrix products, apply_table(): return jnp.einsum(pattern, table, field, precision=lax.Precision.HIGH)  21.1 us
    add x2, other arithmetic, local(): path.append(sum(terms[1:], terms[0]))  16 us
    all_to_all x2, starting transfers between devices, local(): gathered = lax.all_to_all(solved, 'gz', split_axis=0, concat_axis=0)  10.8 us
  transfers between devices with their start and end apart: 12, of which 7 were waited for; matrix products, arithmetic and copies ran while one was open for 19% of the time, Pallas kernels for 0%

profile of v1, /device:TPU:1, one launch (start us, length us, event | category | flops | bytes accessed | tf_op | source)
XLA Modules:
  0.0 274.4 jit_solution(9294311038426620718)
XLA Ops:
  2.7 5.1 %collective-permute-start = (f32[2,4,1,128,128]{4,3,0,2,1:T(8,128)S(1)}, f32[2,4,1,128,128]{4,3,0,2,1:T(8,128)S(1)}, u32[]{:S(2)}, u32[]{:S(2)}) collective-permute-start(f32[2,4,1,128,128]{4,3,0,2,1:T(8,128)S(1)} %pad_maximum_fusion.1), channel_id=1, source_target_pairs={{0,7},{1,0},{2,1},{3,2},{4,3},{5,4},{6,5},{7,6},{8,15},{9,8},{10,9... | collective-permute-start | bytes 1572872 | tf_op jit(solution)/shard_map/ppermute | solution.py:24
  8.8 4.1 %collective-permute-start.2 = (f32[2,4,1,128,128]{4,3,0,2,1:T(8,128)}, f32[2,4,1,128,128]{4,3,0,2,1:T(8,128)}, u32[]{:S(2)}, u32[]{:S(2)}) collective-permute-start(f32[2,4,1,128,128]{4,3,0,2,1:T(8,128)} %pad_maximum_fusion.3), channel_id=1, source_target_pairs={{0,7},{1,0},{2,1},{3,2},{4,3},{5,4},{6,5},{7,6},{8,15},{9,8},{10,9... | collective-permute-start | bytes 1572872 | tf_op jit(solution)/shard_map/ppermute | solution.py:24
  18.1 20.8 %collective-permute-done = f32[2,4,1,128,128]{4,3,0,2,1:T(8,128)S(1)} collective-permute-done((f32[2,4,1,128,128]{4,3,0,2,1:T(8,128)S(1)}, f32[2,4,1,128,128]{4,3,0,2,1:T(8,128)S(1)}, u32[]{:S(2)}, u32[]{:S(2)}) %collective-permute-start) | collective-permute-done | bytes 524320 | tf_op jit(solution)/shard_map/ppermute | solution.py:24
  46.1 4.6 %all-to-all-start = ((f32[8,2,5,2,16,128]{5,4,3,2,1,0:T(8,128)}), f32[8,2,5,2,16,128]{5,4,3,2,1,0:T(8,128)}, u32[]{:S(2)}, u32[]{:S(2)}) async-start(f32[8,2,5,2,16,128]{5,4,3,2,1,0:T(8,128)} %convolution_bitcast_fusion.4), calls=%async_computation | async-start | bytes 2621440 | tf_op jit(solution)/shard_map/all_to_all | solution.py:137
  61.2 18.8 %all-to-all-done = f32[8,2,5,2,16,128]{5,4,3,2,1,0:T(8,128)} async-done(((f32[8,2,5,2,16,128]{5,4,3,2,1,0:T(8,128)}), f32[8,2,5,2,16,128]{5,4,3,2,1,0:T(8,128)}, u32[]{:S(2)}, u32[]{:S(2)}) %all-to-all-start) | async-done | bytes 1310752 | tf_op jit(solution)/shard_map/all_to_all | solution.py:137
  80.0 5.6 %all-to-all-start.2 = ((f32[8,2,5,2,16,128]{5,4,3,2,1,0:T(8,128)}), f32[8,2,5,2,16,128]{5,4,3,2,1,0:T(8,128)}, u32[]{:S(2)}, u32[]{:S(2)}) async-start(f32[8,2,5,2,16,128]{5,4,3,2,1,0:T(8,128)} %convolution_bitcast_fusion.1), calls=%async_computation.2 | async-start | bytes 2621440 | tf_op jit(solution)/shard_map/all_to_all | solution.py:137
  85.9 2.7 fusion.1
  90.8 24.4 %all-to-all-done.2 = f32[8,2,5,2,16,128]{5,4,3,2,1,0:T(8,128)} async-done(((f32[8,2,5,2,16,128]{5,4,3,2,1,0:T(8,128)}), f32[8,2,5,2,16,128]{5,4,3,2,1,0:T(8,128)}, u32[]{:S(2)}, u32[]{:S(2)}) %all-to-all-start.2) | async-done | bytes 1310752 | tf_op jit(solution)/shard_map/all_to_all | solution.py:137
  115.3 5.6 %all-to-all-start.1 = ((f32[8,2,5,2,16,128]{5,4,3,2,1,0:T(8,128)}), f32[8,2,5,2,16,128]{5,4,3,2,1,0:T(8,128)}, u32[]{:S(2)}, u32[]{:S(2)}) async-start(f32[8,2,5,2,16,128]{5,4,3,2,1,0:T(8,128)} %copy.90), calls=%async_computation.1 | async-start | bytes 2621440 | tf_op jit(solution)/shard_map/all_to_all | solution.py:140
  120.8 2.7 fusion.3
  125.8 25.0 %all-to-all-done.1 = f32[8,2,5,2,16,128]{5,4,3,2,1,0:T(8,128)} async-done(((f32[8,2,5,2,16,128]{5,4,3,2,1,0:T(8,128)}), f32[8,2,5,2,16,128]{5,4,3,2,1,0:T(8,128)}, u32[]{:S(2)}, u32[]{:S(2)}) %all-to-all-start.1) | async-done | bytes 1310752 | tf_op jit(solution)/shard_map/all_to_all | solution.py:140
  150.8 5.2 %all-to-all-start.3 = ((f32[8,2,5,2,16,128]{5,4,3,2,1,0:T(8,128)}), f32[8,2,5,2,16,128]{5,4,3,2,1,0:T(8,128)}, u32[]{:S(2)}, u32[]{:S(2)}) async-start(f32[8,2,5,2,16,128]{5,4,3,2,1,0:T(8,128)} %copy.114), calls=%async_computation.3 | async-start | bytes 2621440 | tf_op jit(solution)/shard_map/all_to_all | solution.py:140
  156.1 2.7 convolution_bitcast_fusion.3
  162.1 3.5 %collective-permute-start.4 = (f32[1,5,2,128,128]{4,3,2,1,0:T(8,128)}, f32[1,5,2,128,128]{4,3,2,1,0:T(8,128)S(1)}, u32[]{:S(2)}, u32[]{:S(2)}) collective-permute-start(f32[1,5,2,128,128]{4,3,2,1,0:T(8,128)} %slice.703), channel_id=1, source_target_pairs={{8,0},{16,8},{24,16},{9,1},{17,9},{25,17},{10,2},{18,10},{26,18},{... | collective-permute-start | bytes 1966088 | tf_op jit(solution)/shard_map/ppermute | solution.py:24
  165.6 20.5 %all-to-all-done.3 = f32[8,2,5,2,16,128]{5,4,3,2,1,0:T(8,128)} async-done(((f32[8,2,5,2,16,128]{5,4,3,2,1,0:T(8,128)}), f32[8,2,5,2,16,128]{5,4,3,2,1,0:T(8,128)}, u32[]{:S(2)}, u32[]{:S(2)}) %all-to-all-start.3) | async-done | bytes 1310752 | tf_op jit(solution)/shard_map/all_to_all | solution.py:140
  186.1 2.7 convolution_bitcast_fusion
  190.2 2.1 multiply_reduce_fusion.3
  192.3 5.6 %collective-permute-start.5 = (f32[1,5,2,128,128]{4,3,2,1,0:T(8,128)}, f32[1,5,2,128,128]{4,3,2,1,0:T(8,128)}, u32[]{:S(2)}, u32[]{:S(2)}) collective-permute-start(f32[1,5,2,128,128]{4,3,2,1,0:T(8,128)} %get-tuple-element.45), channel_id=1, source_target_pairs={{0,8},{8,16},{16,24},{1,9},{9,17},{17,25},{2,10},{10,18},{18,26},{... | collective-permute-start | bytes 1966088 | tf_op jit(solution)/shard_map/ppermute | solution.py:24
  197.9 2.6 pad_maximum_fusion.21
  202.5 40.0 %psum.7 = f32[16]{0:T(128)S(1)} all-reduce(f32[16]{0:T(128)S(1)} %compare_select_fusion), channel_id=1, replica_groups=mesh['img'=4,'gz'=8] {'img','gz'}, use_global_device_ids=true, to_apply=%region_4.5 | all-reduce | flops 16 | bytes 128 | tf_op jit(solution)/shard_map/psum | solution.py:160
  243.2 3.4 %collective-permute-start.7 = (f32[1,5,2,128,128]{4,3,2,1,0:T(8,128)S(1)}, f32[1,5,2,128,128]{4,3,2,1,0:T(8,128)S(1)}, u32[]{:S(2)}, u32[]{:S(2)}) collective-permute-start(f32[1,5,2,128,128]{4,3,2,1,0:T(8,128)S(1)} %get-tuple-element.46), channel_id=1, source_target_pairs={{8,0},{16,8},{24,16},{9,1},{17,9},{25,17},{10,2},{18,10},{26,18},{... | collective-permute-start | bytes 1966088 | tf_op jit(solution)/shard_map/ppermute | solution.py:24
  248.9 7.9 %collective-permute-done.7 = f32[1,5,2,128,128]{4,3,2,1,0:T(8,128)S(1)} collective-permute-done((f32[1,5,2,128,128]{4,3,2,1,0:T(8,128)S(1)}, f32[1,5,2,128,128]{4,3,2,1,0:T(8,128)S(1)}, u32[]{:S(2)}, u32[]{:S(2)}) %collective-permute-start.7) | collective-permute-done | bytes 655392 | tf_op jit(solution)/shard_map/ppermute | solution.py:24
  256.7 7.9 %multiply_add_fusion.1 = (f32[1,5,2,128,128]{4,3,2,1,0:T(8,128)S(1)}, f32[1,5,2,128,128]{4,3,2,1,0:T(8,128)S(1)}) fusion(f32[1,5,2,128,128]{4,3,2,1,0:T(8,128)S(1)} %collective-permute-done.4, f32[]{:T(128)} %bitcast.101, f32[]{:T(128)} %bitcast.100, f32[]{:T(128)} %bitcast.99, f32[]{:T(128)} %bitcast.98, f32[]{:T(128)} %bitcast.97, ...), kind=kLoop, calls=%fused_computation.25 | loop fusion | flops 2949120 | bytes 5242920 | tf_op jit(solution)/shard_map/add | solution.py:170
  264.7 8.0 %multiply_add_fusion.3 = (f32[1,5,2,128,128]{4,3,2,1,0:T(8,128)S(1)}, f32[1,5,2,128,128]{4,3,2,1,0:T(8,128)S(1)}) fusion(f32[1,5,2,128,128]{4,3,2,1,0:T(8,128)} %collective-permute-done.6, f32[1,5,2,128,128]{4,3,2,1,0:T(8,128)} %collective-permute-done.5, f32[]{:T(128)} %bitcast.91, f32[]{:T(128)} %bitcast.90, f32[]{:T(128)} %bitcast.89, f32[]{:T(128)} %bitcast.88, ...), kind=kLoop, calls=%fused_computation.27 | loop fusion | flops 2949120 | bytes 5242920 | tf_op jit(solution)/shard_map/add | solution.py:170
  (123 shorter events, 42.3 us)
Async XLA Ops:
  0.0 2.6 copy-start
  2.7 36.2 %collective-permute-start = (f32[2,4,1,128,128]{4,3,0,2,1:T(8,128)S(1)}, f32[2,4,1,128,128]{4,3,0,2,1:T(8,128)S(1)}, u32[]{:S(2)}, u32[]{:S(2)}) collective-permute-start(f32[2,4,1,128,128]{4,3,0,2,1:T(8,128)S(1)} %pad_maximum_fusion.1), channel_id=1, source_target_pairs={{0,7},{1,0},{2,1},{3,2},{4,3},{5,4},{6,5},{7,6},{8,15},{9,8},{10,9... | collective-permute-start | bytes 1572872 | tf_op jit(solution)/shard_map/ppermute | solution.py:24
  7.9 31.9 %collective-permute-start.1 = (f32[2,4,1,128,128]{4,3,0,2,1:T(8,128)S(1)}, f32[2,4,1,128,128]{4,3,0,2,1:T(8,128)S(1)}, u32[]{:S(2)}, u32[]{:S(2)}) collective-permute-start(f32[2,4,1,128,128]{4,3,0,2,1:T(8,128)S(1)} %pad_maximum_fusion.2), channel_id=1, source_target_pairs={{0,1},{1,2},{2,3},{3,4},{4,5},{5,6},{6,7},{7,0},{8,9},{9,10},{10,1... | collective-permute-start | bytes 1572872 | tf_op jit(solution)/shard_map/ppermute | solution.py:24
  8.8 42.2 %collective-permute-start.2 = (f32[2,4,1,128,128]{4,3,0,2,1:T(8,128)}, f32[2,4,1,128,128]{4,3,0,2,1:T(8,128)}, u32[]{:S(2)}, u32[]{:S(2)}) collective-permute-start(f32[2,4,1,128,128]{4,3,0,2,1:T(8,128)} %pad_maximum_fusion.3), channel_id=1, source_target_pairs={{0,7},{1,0},{2,1},{3,2},{4,3},{5,4},{6,5},{7,6},{8,15},{9,8},{10,9... | collective-permute-start | bytes 1572872 | tf_op jit(solution)/shard_map/ppermute | solution.py:24
  13.8 38.6 %collective-permute-start.3 = (f32[2,4,1,128,128]{4,3,0,2,1:T(8,128)}, f32[2,4,1,128,128]{4,3,0,2,1:T(8,128)}, u32[]{:S(2)}, u32[]{:S(2)}) collective-permute-start(f32[2,4,1,128,128]{4,3,0,2,1:T(8,128)} %pad_maximum_fusion.4), channel_id=1, source_target_pairs={{0,1},{1,2},{2,3},{3,4},{4,5},{5,6},{6,7},{7,0},{8,9},{9,10},{10,1... | collective-permute-start | bytes 1572872 | tf_op jit(solution)/shard_map/ppermute | solution.py:24
  46.1 33.8 %all-to-all-start = ((f32[8,2,5,2,16,128]{5,4,3,2,1,0:T(8,128)}), f32[8,2,5,2,16,128]{5,4,3,2,1,0:T(8,128)}, u32[]{:S(2)}, u32[]{:S(2)}) async-start(f32[8,2,5,2,16,128]{5,4,3,2,1,0:T(8,128)} %convolution_bitcast_fusion.4), calls=%async_computation | async-start | bytes 2621440 | tf_op jit(solution)/shard_map/all_to_all | solution.py:137
  52.3 1.3 copy-start.13
  52.3 1.3 copy-start.14
  55.1 1.1 copy-start.11
  55.1 1.2 copy-start.12
  80.0 35.3 %all-to-all-start.2 = ((f32[8,2,5,2,16,128]{5,4,3,2,1,0:T(8,128)}), f32[8,2,5,2,16,128]{5,4,3,2,1,0:T(8,128)}, u32[]{:S(2)}, u32[]{:S(2)}) async-start(f32[8,2,5,2,16,128]{5,4,3,2,1,0:T(8,128)} %convolution_bitcast_fusion.1), calls=%async_computation.2 | async-start | bytes 2621440 | tf_op jit(solution)/shard_map/all_to_all | solution.py:137
  115.3 35.6 %all-to-all-start.1 = ((f32[8,2,5,2,16,128]{5,4,3,2,1,0:T(8,128)}), f32[8,2,5,2,16,128]{5,4,3,2,1,0:T(8,128)}, u32[]{:S(2)}, u32[]{:S(2)}) async-start(f32[8,2,5,2,16,128]{5,4,3,2,1,0:T(8,128)} %copy.90), calls=%async_computation.1 | async-start | bytes 2621440 | tf_op jit(solution)/shard_map/all_to_all | solution.py:140
  150.8 35.3 %all-to-all-start.3 = ((f32[8,2,5,2,16,128]{5,4,3,2,1,0:T(8,128)}), f32[8,2,5,2,16,128]{5,4,3,2,1,0:T(8,128)}, u32[]{:S(2)}, u32[]{:S(2)}) async-start(f32[8,2,5,2,16,128]{5,4,3,2,1,0:T(8,128)} %copy.114), calls=%async_computation.3 | async-start | bytes 2621440 | tf_op jit(solution)/shard_map/all_to_all | solution.py:140
  160.1 1.1 copy-start.1
  161.2 4.4 %copy-start.15 = (s32[4]{0:T(128)S(1)}, s32[4]{0:T(128)}, u32[]{:S(2)}) copy-start(s32[4]{0:T(128)} %param.4) | copy-start | bytes 52
  162.1 28.1 %collective-permute-start.4 = (f32[1,5,2,128,128]{4,3,2,1,0:T(8,128)}, f32[1,5,2,128,128]{4,3,2,1,0:T(8,128)S(1)}, u32[]{:S(2)}, u32[]{:S(2)}) collective-permute-start(f32[1,5,2,128,128]{4,3,2,1,0:T(8,128)} %slice.703), channel_id=1, source_target_pairs={{8,0},{16,8},{24,16},{9,1},{17,9},{25,17},{10,2},{18,10},{26,18},{... | collective-permute-start | bytes 1966088 | tf_op jit(solution)/shard_map/ppermute | solution.py:24
  188.8 1.4 copy-start.2
  190.2 2.1 copy-start.4
  190.2 56.6 %copy-start.16 = (f32[4]{0:T(128)S(1)}, f32[4]{0:T(128)}, u32[]{:S(2)}) copy-start(f32[4]{0:T(128)} %param.5) | copy-start | bytes 52
  190.2 66.5 %copy-start.3 = (f32[2,5,2,128,128]{4,3,2,1,0:T(8,128)S(1)}, f32[2,5,2,128,128]{4,3,2,1,0:T(8,128)}, u32[]{:S(2)}) copy-start(f32[2,5,2,128,128]{4,3,2,1,0:T(8,128)} %copy-done.1) | copy-start | bytes 3932164
  192.3 72.3 %collective-permute-start.5 = (f32[1,5,2,128,128]{4,3,2,1,0:T(8,128)}, f32[1,5,2,128,128]{4,3,2,1,0:T(8,128)}, u32[]{:S(2)}, u32[]{:S(2)}) collective-permute-start(f32[1,5,2,128,128]{4,3,2,1,0:T(8,128)} %get-tuple-element.45), channel_id=1, source_target_pairs={{0,8},{8,16},{16,24},{1,9},{9,17},{17,25},{2,10},{10,18},{18,26},{... | collective-permute-start | bytes 1966088 | tf_op jit(solution)/shard_map/ppermute | solution.py:24
  200.6 64.1 %collective-permute-start.6 = (f32[1,5,2,128,128]{4,3,2,1,0:T(8,128)}, f32[1,5,2,128,128]{4,3,2,1,0:T(8,128)}, u32[]{:S(2)}, u32[]{:S(2)}) collective-permute-start(f32[1,5,2,128,128]{4,3,2,1,0:T(8,128)} %get-tuple-element.47), channel_id=1, source_target_pairs={{0,8},{8,16},{16,24},{1,9},{9,17},{17,25},{2,10},{10,18},{18,26},{... | collective-permute-start | bytes 1966088 | tf_op jit(solution)/shard_map/ppermute | solution.py:24
  243.2 13.5 %collective-permute-start.7 = (f32[1,5,2,128,128]{4,3,2,1,0:T(8,128)S(1)}, f32[1,5,2,128,128]{4,3,2,1,0:T(8,128)S(1)}, u32[]{:S(2)}, u32[]{:S(2)}) collective-permute-start(f32[1,5,2,128,128]{4,3,2,1,0:T(8,128)S(1)} %get-tuple-element.46), channel_id=1, source_target_pairs={{8,0},{16,8},{24,16},{9,1},{17,9},{25,17},{10,2},{18,10},{26,18},{... | collective-permute-start | bytes 1966088 | tf_op jit(solution)/shard_map/ppermute | solution.py:24
  256.7 8.0 %copy-start.5 = (f32[2,5,2,128,128]{4,3,2,1,0:T(8,128)S(1)}, f32[2,5,2,128,128]{4,3,2,1,0:T(8,128)}, u32[]{:S(2)}) copy-start(f32[2,5,2,128,128]{4,3,2,1,0:T(8,128)} %copy-done.4) | copy-start | bytes 3932164
  (5 other events, 4.9 us)

commit v2 on v1

--- a/solution.py
+++ b/solution.py
@@ -3,6 +3,8 @@
 import jax
 import jax.numpy as jnp
 from jax import lax
+from jax.experimental import pallas as pl
+from jax.experimental.pallas import tpu as pltpu
 from jax.sharding import PartitionSpec as P
 
 elastic = 1.0
@@ -142,33 +144,61 @@
         update = apply_table(cas_y, update, "ky,abzxk->abzxy")
         stepped.append((1.0 - step_size * elastic / smoothing) * piece + update)
 
-    single = [part[i : i + 1] for part in stepped for i in range(each)]
     reach = 2
-    right = [shift_along(single[i], "img", -1, False) for i in range(reach)]
-    left = [shift_along(single[count_img - reach + i], "img", 1, False) for i in range(reach)]
-    extended = left + single + right
+    first, last = (stepped[0], stepped[-1]) if each >= reach else (jnp.concatenate(stepped),) * 2
+    right = shift_along(first[:reach], "img", -1, False)
+    left = shift_along(last[last.shape[0] - reach :], "img", 1, False)
+    single = [part[i] for part in stepped for i in range(each)] + [right[0]]
 
     total_images = count_img * lax.axis_size("img")
     first_image = lax.axis_index("img") * count_img
     pair_sums = []
     for i in range(count_img):
-        gap = extended[reach + i + 1] - extended[reach + i]
+        gap = single[i + 1] - single[i]
         pair_sums.append(jnp.sum(gap * gap))
-    sums = jnp.stack(pair_sums)
+    devices = lax.axis_size("img") * groups
+    sums = jnp.broadcast_to(jnp.stack(pair_sums)[None, :], (devices, count_img))
+    sums = lax.all_to_all(sums, ("img", "gz"), split_axis=0, concat_axis=0, tiled=True)
+    totals = jnp.sum(sums.reshape(-1, groups, count_img), axis=1).reshape(-1)
+    cells = 5.0 * depth * width_x * width_y
     global_index = jnp.arange(total_images, dtype=jnp.int32)
-    own = global_index // count_img == lax.axis_index("img")
-    totals = lax.psum(jnp.where(own, jnp.tile(sums, lax.axis_size("img")), 0.0), ("img", "gz"))
-    cells = 5.0 * depth * width_x * width_y
     dist = jnp.where(global_index < total_images - 1, jnp.sqrt(totals / cells + epsilon), 0.0)
     earlier = global_index[None, :] < global_index[:, None]
     arc = jnp.sum(jnp.where(earlier, dist[None, :], 0.0), axis=1)
     target = positions * jnp.sum(dist)
     matrix = interp_matrix(arc, centre, target, count_img + 2 * reach, first_image - reach)
-    path = []
-    for m in range(count_img):
-        terms = [matrix[m, m + d] * extended[m + d] for d in range(2 * reach + 1)]
-        path.append(sum(terms[1:], terms[0]))
-    return jnp.concatenate(path, axis=0)
+    return mix(matrix, [left] + stepped + [right], images)
+
+
+def mix_kernel(matrix, *refs):
+    *sources, path = refs
+    nodes = [source.at[i] for source in sources for i in range(source.shape[0])]
+    taken = len(nodes) - path.shape[0] + 1
+    for m in range(path.shape[0]):
+        total = matrix[m, m] * nodes[m][...]
+        for d in range(1, taken):
+            total = total + matrix[m, m + d] * nodes[m + d][...]
+        path[m] = total
+
+
+def mix(matrix, sources, like):
+    def block(array):
+        return pl.BlockSpec(
+            (array.shape[0], 1) + array.shape[2:], lambda slot: (0, slot, 0, 0, 0)
+        )
+
+    return pl.pallas_call(
+        mix_kernel,
+        grid=(like.shape[1],),
+        in_specs=[pl.BlockSpec(memory_space=pltpu.SMEM)] + [block(s) for s in sources],
+        out_specs=block(like),
+        out_shape=jax.ShapeDtypeStruct(like.shape, like.dtype),
+        compiler_params=pltpu.CompilerParams(vmem_limit_bytes=32 * 2**20),
+        cost_estimate=pl.CostEstimate(
+            flops=10 * like.size, bytes_accessed=12 * like.size, transcendentals=0
+        ),
+        name="mix",
+    )(matrix, *sources)
 
 
 def solution(mesh):

time: 275 us -> 217 us (0.79)
  blocking collectives: 40 us -> 0 us
  other arithmetic: 30.9 us -> 13.3 us
  starting transfers between devices: 44.7 us -> 39.6 us
  Pallas kernels: 0 us -> 5.1 us
  waiting for transfers between devices: 118 us -> 122 us
    psum x1 -> x0, blocking collectives: 40 us -> none  [local(): lax.psum(jnp.where(own, jnp.tile(sums, lax.axis_size('img')), 0.0), ('img...]
    add x2 -> x0, other arithmetic: 16 us -> none  [local(): path.append(sum(terms[1:], terms[0]))]
    ppermute x8 -> x6, waiting for transfers between devices: 29.5 us -> 21.6 us  [shift_along(): return lax.ppermute(block, axis, pairs)]
    ppermute x8 -> x6, starting transfers between devices: 23.7 us -> 16.8 us  [shift_along(): return lax.ppermute(block, axis, pairs)]
    all_to_all x0 -> x1, waiting for transfers between devices: none -> 6.85 us  [local(): lax.all_to_all(sums, ('img', 'gz'), split_axis=0, concat_axis=0, tiled=True)]
    pallas_call x0 -> x1, Pallas kernels: none -> 5.1 us  [mix(): pl.pallas_call(mix_kernel, grid=(like.shape[1],), in_specs=[pl.BlockSpec(...]
    all_to_all x2, waiting for transfers between devices: 45.5 us -> 50 us  [local(): gathered = lax.all_to_all(solved, 'gz', split_axis=0, concat_axis=0)]
  transfers between devices with their start and end apart: 12 -> 11, of which waited for: 7 -> 7; matrix products, arithmetic and copies ran while one was open for 19% -> 20% of each run, Pallas kernels for 0% -> 0%
where the time goes in v2:
time: 217 us; the launch traced here: 216 us
  waiting for transfers between devices  122 us (56%)
  starting transfers between devices  39.6 us (18%)
  matrix products  18.6 us (9%)
  local copies, waits for them, and re-layouts  16.8 us (8%)
  other arithmetic  13.3 us (6%)
  Pallas kernels  5.1 us (2%)
    all_to_all x2, waiting for transfers between devices, local(): gathered = lax.all_to_all(solved, 'gz', split_axis=0, concat_axis=0)  50 us
    all_to_all x2, waiting for transfers between devices, local(): lines = lax.all_to_all(spread, 'gz', split_axis=0, concat_axis=0)  43.9 us
    ppermute x6, waiting for transfers between devices, shift_along(): return lax.ppermute(block, axis, pairs)  21.6 us
    dot_general x12, matrix products, apply_table(): return jnp.einsum(pattern, table, field, precision=lax.Precision.HIGH)  18.6 us
    ppermute x6, starting transfers between devices, shift_along(): return lax.ppermute(block, axis, pairs)  16.8 us
    all_to_all x2, starting transfers between devices, local(): lines = lax.all_to_all(spread, 'gz', split_axis=0, concat_axis=0)  10.2 us
    all_to_all x2, starting transfers between devices, local(): gathered = lax.all_to_all(solved, 'gz', split_axis=0, concat_axis=0)  10.1 us
    all_to_all x1, waiting for transfers between devices, local(): lax.all_to_all(sums, ('img', 'gz'), split_axis=0, concat_axis=0, tiled=True)  6.85 us
  transfers between devices with their start and end apart: 11, of which 7 were waited for; matrix products, arithmetic and copies ran while one was open for 20% of the time, Pallas kernels for 0%

profile of v2, /device:TPU:1, one launch (start us, length us, event | category | flops | bytes accessed | tf_op | source)
XLA Modules:
  0.0 216.3 jit_solution(9804169160258250643)
XLA Ops:
  2.7 5.1 %collective-permute-start = (f32[2,4,1,128,128]{4,3,0,2,1:T(8,128)S(1)}, f32[2,4,1,128,128]{4,3,0,2,1:T(8,128)S(1)}, u32[]{:S(2)}, u32[]{:S(2)}) collective-permute-start(f32[2,4,1,128,128]{4,3,0,2,1:T(8,128)S(1)} %pad_maximum_fusion), channel_id=1, source_target_pairs={{0,7},{1,0},{2,1},{3,2},{4,3},{5,4},{6,5},{7,6},{8,15},{9,8},{10,9... | collective-permute-start | bytes 1572872 | tf_op jit(solution)/shard_map/ppermute | solution.py:26
  8.8 4.1 %collective-permute-start.2 = (f32[2,4,1,128,128]{4,3,0,2,1:T(8,128)}, f32[2,4,1,128,128]{4,3,0,2,1:T(8,128)}, u32[]{:S(2)}, u32[]{:S(2)}) collective-permute-start(f32[2,4,1,128,128]{4,3,0,2,1:T(8,128)} %pad_maximum_fusion.2), channel_id=1, source_target_pairs={{0,7},{1,0},{2,1},{3,2},{4,3},{5,4},{6,5},{7,6},{8,15},{9,8},{10,9... | collective-permute-start | bytes 1572872 | tf_op jit(solution)/shard_map/ppermute | solution.py:26
  18.1 20.8 %collective-permute-done = f32[2,4,1,128,128]{4,3,0,2,1:T(8,128)S(1)} collective-permute-done((f32[2,4,1,128,128]{4,3,0,2,1:T(8,128)S(1)}, f32[2,4,1,128,128]{4,3,0,2,1:T(8,128)S(1)}, u32[]{:S(2)}, u32[]{:S(2)}) %collective-permute-start) | collective-permute-done | bytes 524320 | tf_op jit(solution)/shard_map/ppermute | solution.py:26
  44.1 2.1 convolution_bitcast_fusion.4
  46.1 4.6 %all-to-all-start = ((f32[8,2,5,2,16,128]{5,4,3,2,1,0:T(8,128)}), f32[8,2,5,2,16,128]{5,4,3,2,1,0:T(8,128)}, u32[]{:S(2)}, u32[]{:S(2)}) async-start(f32[8,2,5,2,16,128]{5,4,3,2,1,0:T(8,128)} %convolution_bitcast_fusion.4), calls=%async_computation | async-start | bytes 2621440 | tf_op jit(solution)/shard_map/all_to_all | solution.py:139
  59.1 2.1 convolution_bitcast_fusion.1
  61.2 18.8 %all-to-all-done = f32[8,2,5,2,16,128]{5,4,3,2,1,0:T(8,128)} async-done(((f32[8,2,5,2,16,128]{5,4,3,2,1,0:T(8,128)}), f32[8,2,5,2,16,128]{5,4,3,2,1,0:T(8,128)}, u32[]{:S(2)}, u32[]{:S(2)}) %all-to-all-start) | async-done | bytes 1310752 | tf_op jit(solution)/shard_map/all_to_all | solution.py:139
  80.0 5.6 %all-to-all-start.2 = ((f32[8,2,5,2,16,128]{5,4,3,2,1,0:T(8,128)}), f32[8,2,5,2,16,128]{5,4,3,2,1,0:T(8,128)S(1)}, u32[]{:S(2)}, u32[]{:S(2)}) async-start(f32[8,2,5,2,16,128]{5,4,3,2,1,0:T(8,128)} %convolution_bitcast_fusion.1), calls=%async_computation.2 | async-start | bytes 2621440 | tf_op jit(solution)/shard_map/all_to_all | solution.py:139
  85.9 2.7 %fusion.1 = f32[16,2,5,16,128,1]{4,0,5,3,2,1:T(8,128)S(1)} fusion(f32[8,2,5,2,16,128]{5,4,3,2,1,0:T(8,128)} %all-to-all-done, f32[16,16,128]{2,0,1:T(8,128)S(1)} %multiply_divide_fusion, s32[8,2]{0,1:T(2,128)S(1)} %multiply_add_fusion.5), kind=kOutput, calls=%fused_computation.13 | convolution fusion | flops 31788800 | bytes 2752576 | tf_op jit(solution)/shard_map/wgz,gabzky->wabky/dot_general | solution.py:88
  89.4 1.5 copy.92
  90.8 25.1 %all-to-all-done.2 = f32[8,2,5,2,16,128]{5,4,3,2,1,0:T(8,128)S(1)} async-done(((f32[8,2,5,2,16,128]{5,4,3,2,1,0:T(8,128)}), f32[8,2,5,2,16,128]{5,4,3,2,1,0:T(8,128)S(1)}, u32[]{:S(2)}, u32[]{:S(2)}) %all-to-all-start.2) | async-done | bytes 1310752 | tf_op jit(solution)/shard_map/all_to_all | solution.py:139
  115.9 4.8 %all-to-all-start.1 = ((f32[8,2,5,2,16,128]{5,4,3,2,1,0:T(8,128)}), f32[8,2,5,2,16,128]{5,4,3,2,1,0:T(8,128)}, u32[]{:S(2)}, u32[]{:S(2)}) async-start(f32[8,2,5,2,16,128]{5,4,3,2,1,0:T(8,128)} %copy.92), calls=%async_computation.1 | async-start | bytes 2621440 | tf_op jit(solution)/shard_map/all_to_all | solution.py:142
  122.9 1.5 copy.116
  124.4 26.3 %all-to-all-done.1 = f32[8,2,5,2,16,128]{5,4,3,2,1,0:T(8,128)} async-done(((f32[8,2,5,2,16,128]{5,4,3,2,1,0:T(8,128)}), f32[8,2,5,2,16,128]{5,4,3,2,1,0:T(8,128)}, u32[]{:S(2)}, u32[]{:S(2)}) %all-to-all-start.1) | async-done | bytes 1310752 | tf_op jit(solution)/shard_map/all_to_all | solution.py:142
  150.7 5.3 %all-to-all-start.3 = ((f32[8,2,5,2,16,128]{5,4,3,2,1,0:T(8,128)}), f32[8,2,5,2,16,128]{5,4,3,2,1,0:T(8,128)S(1)}, u32[]{:S(2)}, u32[]{:S(2)}) async-start(f32[8,2,5,2,16,128]{5,4,3,2,1,0:T(8,128)} %copy.116), calls=%async_computation.3 | async-start | bytes 2621440 | tf_op jit(solution)/shard_map/all_to_all | solution.py:142
  156.0 2.8 %convolution_bitcast_fusion.3 = f32[2,5,2,128,128]{3,4,1,0,2:T(8,128)S(1)} fusion(f32[8,2,5,2,16,128]{5,4,3,2,1,0:T(8,128)} %all-to-all-done.1, s32[8,16]{1,0:T(8,128)S(1)} %multiply_add_fusion.4), kind=kOutput, calls=%fused_computation.5 | convolution fusion | flops 251904000 | bytes 2621952 | tf_op jit(solution)/shard_map/gkx,gabzky->abzxy/dot_general | solution.py:88
  160.2 2.8 %collective-permute-start.4 = (f32[2,5,2,128,128]{4,3,2,1,0:T(8,128)S(1)}, f32[2,5,2,128,128]{4,3,2,1,0:T(8,128)}, u32[]{:S(2)}, u32[]{:S(2)}) collective-permute-start(f32[2,5,2,128,128]{4,3,2,1,0:T(8,128)S(1)} %convolution_add_fusion.1.refs_1_), channel_id=1, source_target_pairs={{8,0},{16,8},{24,16},{9,1},{17,9},{25,17},{10,2},{18,10},{26,18},{... | collective-permute-start | bytes 3932168 | tf_op jit(solution)/shard_map/ppermute | solution.py:26
  163.0 23.7 %all-to-all-done.3 = f32[8,2,5,2,16,128]{5,4,3,2,1,0:T(8,128)S(1)} async-done(((f32[8,2,5,2,16,128]{5,4,3,2,1,0:T(8,128)}), f32[8,2,5,2,16,128]{5,4,3,2,1,0:T(8,128)S(1)}, u32[]{:S(2)}, u32[]{:S(2)}) %all-to-all-start.3) | async-done | bytes 1310752 | tf_op jit(solution)/shard_map/all_to_all | solution.py:142
  189.8 4.7 %collective-permute-start.5 = (f32[2,5,2,128,128]{4,3,2,1,0:T(8,128)S(1)}, f32[2,5,2,128,128]{4,3,2,1,0:T(8,128)}, u32[]{:S(2)}, u32[]{:S(2)}) collective-permute-start(f32[2,5,2,128,128]{4,3,2,1,0:T(8,128)S(1)} %convolution_add_fusion.refs_2_), channel_id=1, source_target_pairs={{0,8},{8,16},{16,24},{1,9},{9,17},{17,25},{2,10},{10,18},{18,26},{... | collective-permute-start | bytes 3932168 | tf_op jit(solution)/shard_map/ppermute | solution.py:26
  194.5 2.1 fusion.14
  196.5 2.6 %pad_maximum_fusion.20 = f32[4]{0:T(128)S(1)} fusion(f32[1]{0:T(128)} %bitcast.86, f32[1]{0:T(128)} %bitcast.85, f32[1]{0:T(128)} %bitcast.84, f32[1]{0:T(128)} %bitcast.45), kind=kLoop, calls=%fused_computation.324 | loop fusion | flops 12 | bytes 32 | tf_op jit(solution)/shard_map/stack | solution.py:160
  199.7 2.6 %all-to-all-start.4 = ((f32[32,1,4]{2,1,0:T(1,128)}), f32[32,1,4]{2,1,0:T(1,128)S(1)}, u32[]{:S(2)}, u32[]{:S(2)}) async-start(f32[32,1,4]{2,1,0:T(1,128)} %broadcast_in_dim.99), calls=%async_computation.4 | async-start | bytes 32768 | tf_op jit(solution)/shard_map/all_to_all | solution.py:161
  202.4 6.9 %all-to-all-done.4 = f32[32,1,4]{2,1,0:T(1,128)S(1)} async-done(((f32[32,1,4]{2,1,0:T(1,128)}), f32[32,1,4]{2,1,0:T(1,128)S(1)}, u32[]{:S(2)}, u32[]{:S(2)}) %all-to-all-start.4) | async-done | bytes 544 | tf_op jit(solution)/shard_map/all_to_all | solution.py:161
  211.2 5.1 %mix.1 = f32[4,5,2,128,128]{4,3,2,1,0:T(8,128)} custom-call(f32[4,8]{1,0:T(4,128)S(1)} %select_add_fusion.matrix, f32[2,5,2,128,128]{4,3,2,1,0:T(8,128)} %collective-permute-done.5.refs_0_, f32[2,5,2,128,128]{4,3,2,1,0:T(8,128)S(1)} %convolution_add_fusion.1.refs_1_, f32[2,5,2,128,128]{4,3,2,1,0:T(8,128)S(1)} %convolution_add_fusion.refs_2_, ...), custom_call_target="tpu_custom_call" | custom-call | flops 6553600 | bytes 7864320 | tf_op jit(solution)/shard_map/mix/pallas_call | solution.py:190
  (112 shorter events, 32.4 us)
Async XLA Ops:
  0.0 2.6 %copy-start = (f32[4,5,2,128,128]{4,3,2,1,0:T(8,128)S(1)}, f32[4,5,2,128,128]{4,3,2,1,0:T(8,128)}, u32[]{:S(2)}) copy-start(f32[4,5,2,128,128]{4,3,2,1,0:T(8,128)} %param.3) | copy-start | bytes 7864324
  2.7 36.2 %collective-permute-start = (f32[2,4,1,128,128]{4,3,0,2,1:T(8,128)S(1)}, f32[2,4,1,128,128]{4,3,0,2,1:T(8,128)S(1)}, u32[]{:S(2)}, u32[]{:S(2)}) collective-permute-start(f32[2,4,1,128,128]{4,3,0,2,1:T(8,128)S(1)} %pad_maximum_fusion), channel_id=1, source_target_pairs={{0,7},{1,0},{2,1},{3,2},{4,3},{5,4},{6,5},{7,6},{8,15},{9,8},{10,9... | collective-permute-start | bytes 1572872 | tf_op jit(solution)/shard_map/ppermute | solution.py:26
  7.9 31.9 %collective-permute-start.1 = (f32[2,4,1,128,128]{4,3,0,2,1:T(8,128)S(1)}, f32[2,4,1,128,128]{4,3,0,2,1:T(8,128)S(1)}, u32[]{:S(2)}, u32[]{:S(2)}) collective-permute-start(f32[2,4,1,128,128]{4,3,0,2,1:T(8,128)S(1)} %pad_maximum_fusion.1), channel_id=1, source_target_pairs={{0,1},{1,2},{2,3},{3,4},{4,5},{5,6},{6,7},{7,0},{8,9},{9,10},{10,1... | collective-permute-start | bytes 1572872 | tf_op jit(solution)/shard_map/ppermute | solution.py:26
  8.8 42.2 %collective-permute-start.2 = (f32[2,4,1,128,128]{4,3,0,2,1:T(8,128)}, f32[2,4,1,128,128]{4,3,0,2,1:T(8,128)}, u32[]{:S(2)}, u32[]{:S(2)}) collective-permute-start(f32[2,4,1,128,128]{4,3,0,2,1:T(8,128)} %pad_maximum_fusion.2), channel_id=1, source_target_pairs={{0,7},{1,0},{2,1},{3,2},{4,3},{5,4},{6,5},{7,6},{8,15},{9,8},{10,9... | collective-permute-start | bytes 1572872 | tf_op jit(solution)/shard_map/ppermute | solution.py:26
  13.8 38.6 %collective-permute-start.3 = (f32[2,4,1,128,128]{4,3,0,2,1:T(8,128)}, f32[2,4,1,128,128]{4,3,0,2,1:T(8,128)}, u32[]{:S(2)}, u32[]{:S(2)}) collective-permute-start(f32[2,4,1,128,128]{4,3,0,2,1:T(8,128)} %pad_maximum_fusion.3), channel_id=1, source_target_pairs={{0,1},{1,2},{2,3},{3,4},{4,5},{5,6},{6,7},{7,0},{8,9},{9,10},{10,1... | collective-permute-start | bytes 1572872 | tf_op jit(solution)/shard_map/ppermute | solution.py:26
  46.1 33.8 %all-to-all-start = ((f32[8,2,5,2,16,128]{5,4,3,2,1,0:T(8,128)}), f32[8,2,5,2,16,128]{5,4,3,2,1,0:T(8,128)}, u32[]{:S(2)}, u32[]{:S(2)}) async-start(f32[8,2,5,2,16,128]{5,4,3,2,1,0:T(8,128)} %convolution_bitcast_fusion.4), calls=%async_computation | async-start | bytes 2621440 | tf_op jit(solution)/shard_map/all_to_all | solution.py:139
  52.3 1.3 copy-start.10
  52.3 1.3 copy-start.11
  55.1 1.0 copy-start.6
  55.1 1.0 copy-start.7
  55.1 1.1 copy-start.8
  55.1 1.2 copy-start.9
  56.7 1.0 copy-start.4
  56.7 1.0 copy-start.5
  80.0 35.9 %all-to-all-start.2 = ((f32[8,2,5,2,16,128]{5,4,3,2,1,0:T(8,128)}), f32[8,2,5,2,16,128]{5,4,3,2,1,0:T(8,128)S(1)}, u32[]{:S(2)}, u32[]{:S(2)}) async-start(f32[8,2,5,2,16,128]{5,4,3,2,1,0:T(8,128)} %convolution_bitcast_fusion.1), calls=%async_computation.2 | async-start | bytes 2621440 | tf_op jit(solution)/shard_map/all_to_all | solution.py:139
  115.9 34.8 %all-to-all-start.1 = ((f32[8,2,5,2,16,128]{5,4,3,2,1,0:T(8,128)}), f32[8,2,5,2,16,128]{5,4,3,2,1,0:T(8,128)}, u32[]{:S(2)}, u32[]{:S(2)}) async-start(f32[8,2,5,2,16,128]{5,4,3,2,1,0:T(8,128)} %copy.92), calls=%async_computation.1 | async-start | bytes 2621440 | tf_op jit(solution)/shard_map/all_to_all | solution.py:142
  150.7 36.0 %all-to-all-start.3 = ((f32[8,2,5,2,16,128]{5,4,3,2,1,0:T(8,128)}), f32[8,2,5,2,16,128]{5,4,3,2,1,0:T(8,128)S(1)}, u32[]{:S(2)}, u32[]{:S(2)}) async-start(f32[8,2,5,2,16,128]{5,4,3,2,1,0:T(8,128)} %copy.116), calls=%async_computation.3 | async-start | bytes 2621440 | tf_op jit(solution)/shard_map/all_to_all | solution.py:142
  156.0 2.8 %copy-start.1 = (f32[4,5,2,128,128]{4,3,2,1,0:T(8,128)S(1)}, f32[4,5,2,128,128]{4,3,2,1,0:T(8,128)}, u32[]{:S(2)}) copy-start(f32[4,5,2,128,128]{4,3,2,1,0:T(8,128)} %param.3) | copy-start | bytes 7864324
  160.2 34.3 %collective-permute-start.4 = (f32[2,5,2,128,128]{4,3,2,1,0:T(8,128)S(1)}, f32[2,5,2,128,128]{4,3,2,1,0:T(8,128)}, u32[]{:S(2)}, u32[]{:S(2)}) collective-permute-start(f32[2,5,2,128,128]{4,3,2,1,0:T(8,128)S(1)} %convolution_add_fusion.1.refs_1_), channel_id=1, source_target_pairs={{8,0},{16,8},{24,16},{9,1},{17,9},{25,17},{10,2},{18,10},{26,18},{... | collective-permute-start | bytes 3932168 | tf_op jit(solution)/shard_map/ppermute | solution.py:26
  186.7 1.7 copy-start.2
  189.8 12.6 %copy-start.12 = (s32[4]{0:T(128)S(1)}, s32[4]{0:T(128)}, u32[]{:S(2)}) copy-start(s32[4]{0:T(128)} %param.4) | copy-start | bytes 52
  189.8 20.7 %copy-start.13 = (f32[4]{0:T(128)S(1)}, f32[4]{0:T(128)}, u32[]{:S(2)}) copy-start(f32[4]{0:T(128)} %param.5) | copy-start | bytes 52
  189.8 21.4 %collective-permute-start.5 = (f32[2,5,2,128,128]{4,3,2,1,0:T(8,128)S(1)}, f32[2,5,2,128,128]{4,3,2,1,0:T(8,128)}, u32[]{:S(2)}, u32[]{:S(2)}) collective-permute-start(f32[2,5,2,128,128]{4,3,2,1,0:T(8,128)S(1)} %convolution_add_fusion.refs_2_), channel_id=1, source_target_pairs={{0,8},{8,16},{16,24},{1,9},{9,17},{17,25},{2,10},{10,18},{18,26},{... | collective-permute-start | bytes 3932168 | tf_op jit(solution)/shard_map/ppermute | solution.py:26
  199.7 9.5 %all-to-all-start.4 = ((f32[32,1,4]{2,1,0:T(1,128)}), f32[32,1,4]{2,1,0:T(1,128)S(1)}, u32[]{:S(2)}, u32[]{:S(2)}) async-start(f32[32,1,4]{2,1,0:T(1,128)} %broadcast_in_dim.99), calls=%async_computation.4 | async-start | bytes 32768 | tf_op jit(solution)/shard_map/all_to_all | solution.py:161
  (1 other events, 0.9 us)

commit v3 on v2

--- a/solution.py
+++ b/solution.py
@@ -184,12 +184,12 @@
 def mix(matrix, sources, like):
     def block(array):
         return pl.BlockSpec(
-            (array.shape[0], 1) + array.shape[2:], lambda slot: (0, slot, 0, 0, 0)
+            (array.shape[0], 1, 1) + array.shape[3:], lambda slot, z: (0, slot, z, 0, 0)
         )
 
     return pl.pallas_call(
         mix_kernel,
-        grid=(like.shape[1],),
+        grid=like.shape[1:3],
         in_specs=[pl.BlockSpec(memory_space=pltpu.SMEM)] + [block(s) for s in sources],
         out_specs=block(like),
         out_shape=jax.ShapeDtypeStruct(like.shape, like.dtype),

time: 217 us -> 220 us (1.014)
  no operation moved by 1% of the time
where the time goes in v3:
time: 220 us; the launch traced here: 219 us
  waiting for transfers between devices  122 us (55%)
  starting transfers between devices  39.6 us (18%)
  matrix products  18.6 us (8%)
  local copies, waits for them, and re-layouts  16.8 us (8%)
  other arithmetic  13.3 us (6%)
  Pallas kernels  7.29 us (3%)
    all_to_all x2, waiting for transfers between devices, local(): gathered = lax.all_to_all(solved, 'gz', split_axis=0, concat_axis=0)  50 us
    all_to_all x2, waiting for transfers between devices, local(): lines = lax.all_to_all(spread, 'gz', split_axis=0, concat_axis=0)  43.9 us
    ppermute x6, waiting for transfers between devices, shift_along(): return lax.ppermute(block, axis, pairs)  21.6 us
    dot_general x12, matrix products, apply_table(): return jnp.einsum(pattern, table, field, precision=lax.Precision.HIGH)  18.6 us
    ppermute x6, starting transfers between devices, shift_along(): return lax.ppermute(block, axis, pairs)  16.8 us
    all_to_all x2, starting transfers between devices, local(): lines = lax.all_to_all(spread, 'gz', split_axis=0, concat_axis=0)  10.2 us
    all_to_all x2, starting transfers between devices, local(): gathered = lax.all_to_all(solved, 'gz', split_axis=0, concat_axis=0)  10.1 us
    pallas_call x1, Pallas kernels, mix(): pl.pallas_call(mix_kernel, grid=like.shape[1:3], in_specs=[pl.BlockSpec(m...  7.29 us
  transfers between devices with their start and end apart: 11, of which 7 were waited for; matrix products, arithmetic and copies ran while one was open for 20% of the time, Pallas kernels for 0%

profile of v3, /device:TPU:1, one launch (start us, length us, event | category | flops | bytes accessed | tf_op | source)
XLA Modules:
  0.0 218.5 jit_solution(14724336378417771828)
XLA Ops:
  2.7 5.1 %collective-permute-start = (f32[2,4,1,128,128]{4,3,0,2,1:T(8,128)S(1)}, f32[2,4,1,128,128]{4,3,0,2,1:T(8,128)S(1)}, u32[]{:S(2)}, u32[]{:S(2)}) collective-permute-start(f32[2,4,1,128,128]{4,3,0,2,1:T(8,128)S(1)} %pad_maximum_fusion), channel_id=1, source_target_pairs={{0,7},{1,0},{2,1},{3,2},{4,3},{5,4},{6,5},{7,6},{8,15},{9,8},{10,9... | collective-permute-start | bytes 1572872 | tf_op jit(solution)/shard_map/ppermute | solution.py:26
  8.8 4.1 %collective-permute-start.2 = (f32[2,4,1,128,128]{4,3,0,2,1:T(8,128)}, f32[2,4,1,128,128]{4,3,0,2,1:T(8,128)}, u32[]{:S(2)}, u32[]{:S(2)}) collective-permute-start(f32[2,4,1,128,128]{4,3,0,2,1:T(8,128)} %pad_maximum_fusion.2), channel_id=1, source_target_pairs={{0,7},{1,0},{2,1},{3,2},{4,3},{5,4},{6,5},{7,6},{8,15},{9,8},{10,9... | collective-permute-start | bytes 1572872 | tf_op jit(solution)/shard_map/ppermute | solution.py:26
  18.1 20.8 %collective-permute-done = f32[2,4,1,128,128]{4,3,0,2,1:T(8,128)S(1)} collective-permute-done((f32[2,4,1,128,128]{4,3,0,2,1:T(8,128)S(1)}, f32[2,4,1,128,128]{4,3,0,2,1:T(8,128)S(1)}, u32[]{:S(2)}, u32[]{:S(2)}) %collective-permute-start) | collective-permute-done | bytes 524320 | tf_op jit(solution)/shard_map/ppermute | solution.py:26
  44.1 2.1 convolution_bitcast_fusion.4
  46.1 4.6 %all-to-all-start = ((f32[8,2,5,2,16,128]{5,4,3,2,1,0:T(8,128)}), f32[8,2,5,2,16,128]{5,4,3,2,1,0:T(8,128)}, u32[]{:S(2)}, u32[]{:S(2)}) async-start(f32[8,2,5,2,16,128]{5,4,3,2,1,0:T(8,128)} %convolution_bitcast_fusion.4), calls=%async_computation | async-start | bytes 2621440 | tf_op jit(solution)/shard_map/all_to_all | solution.py:139
  59.1 2.1 convolution_bitcast_fusion.1
  61.2 18.8 %all-to-all-done = f32[8,2,5,2,16,128]{5,4,3,2,1,0:T(8,128)} async-done(((f32[8,2,5,2,16,128]{5,4,3,2,1,0:T(8,128)}), f32[8,2,5,2,16,128]{5,4,3,2,1,0:T(8,128)}, u32[]{:S(2)}, u32[]{:S(2)}) %all-to-all-start) | async-done | bytes 1310752 | tf_op jit(solution)/shard_map/all_to_all | solution.py:139
  80.0 5.6 %all-to-all-start.2 = ((f32[8,2,5,2,16,128]{5,4,3,2,1,0:T(8,128)}), f32[8,2,5,2,16,128]{5,4,3,2,1,0:T(8,128)S(1)}, u32[]{:S(2)}, u32[]{:S(2)}) async-start(f32[8,2,5,2,16,128]{5,4,3,2,1,0:T(8,128)} %convolution_bitcast_fusion.1), calls=%async_computation.2 | async-start | bytes 2621440 | tf_op jit(solution)/shard_map/all_to_all | solution.py:139
  85.9 2.7 %fusion.1 = f32[16,2,5,16,128,1]{4,0,5,3,2,1:T(8,128)S(1)} fusion(f32[8,2,5,2,16,128]{5,4,3,2,1,0:T(8,128)} %all-to-all-done, f32[16,16,128]{2,0,1:T(8,128)S(1)} %multiply_divide_fusion, s32[8,2]{0,1:T(2,128)S(1)} %multiply_add_fusion.5), kind=kOutput, calls=%fused_computation.13 | convolution fusion | flops 31788800 | bytes 2752576 | tf_op jit(solution)/shard_map/wgz,gabzky->wabky/dot_general | solution.py:88
  89.4 1.5 copy.92
  90.8 25.1 %all-to-all-done.2 = f32[8,2,5,2,16,128]{5,4,3,2,1,0:T(8,128)S(1)} async-done(((f32[8,2,5,2,16,128]{5,4,3,2,1,0:T(8,128)}), f32[8,2,5,2,16,128]{5,4,3,2,1,0:T(8,128)S(1)}, u32[]{:S(2)}, u32[]{:S(2)}) %all-to-all-start.2) | async-done | bytes 1310752 | tf_op jit(solution)/shard_map/all_to_all | solution.py:139
  115.9 4.8 %all-to-all-start.1 = ((f32[8,2,5,2,16,128]{5,4,3,2,1,0:T(8,128)}), f32[8,2,5,2,16,128]{5,4,3,2,1,0:T(8,128)}, u32[]{:S(2)}, u32[]{:S(2)}) async-start(f32[8,2,5,2,16,128]{5,4,3,2,1,0:T(8,128)} %copy.92), calls=%async_computation.1 | async-start | bytes 2621440 | tf_op jit(solution)/shard_map/all_to_all | solution.py:142
  122.9 1.5 copy.116
  124.4 26.3 %all-to-all-done.1 = f32[8,2,5,2,16,128]{5,4,3,2,1,0:T(8,128)} async-done(((f32[8,2,5,2,16,128]{5,4,3,2,1,0:T(8,128)}), f32[8,2,5,2,16,128]{5,4,3,2,1,0:T(8,128)}, u32[]{:S(2)}, u32[]{:S(2)}) %all-to-all-start.1) | async-done | bytes 1310752 | tf_op jit(solution)/shard_map/all_to_all | solution.py:142
  150.7 5.3 %all-to-all-start.3 = ((f32[8,2,5,2,16,128]{5,4,3,2,1,0:T(8,128)}), f32[8,2,5,2,16,128]{5,4,3,2,1,0:T(8,128)S(1)}, u32[]{:S(2)}, u32[]{:S(2)}) async-start(f32[8,2,5,2,16,128]{5,4,3,2,1,0:T(8,128)} %copy.116), calls=%async_computation.3 | async-start | bytes 2621440 | tf_op jit(solution)/shard_map/all_to_all | solution.py:142
  156.0 2.8 %convolution_bitcast_fusion.3 = f32[2,5,2,128,128]{3,4,1,0,2:T(8,128)S(1)} fusion(f32[8,2,5,2,16,128]{5,4,3,2,1,0:T(8,128)} %all-to-all-done.1, s32[8,16]{1,0:T(8,128)S(1)} %multiply_add_fusion.4), kind=kOutput, calls=%fused_computation.5 | convolution fusion | flops 251904000 | bytes 2621952 | tf_op jit(solution)/shard_map/gkx,gabzky->abzxy/dot_general | solution.py:88
  160.2 2.8 %collective-permute-start.4 = (f32[2,5,2,128,128]{4,3,2,1,0:T(8,128)S(1)}, f32[2,5,2,128,128]{4,3,2,1,0:T(8,128)}, u32[]{:S(2)}, u32[]{:S(2)}) collective-permute-start(f32[2,5,2,128,128]{4,3,2,1,0:T(8,128)S(1)} %convolution_add_fusion.1.refs_1_), channel_id=1, source_target_pairs={{8,0},{16,8},{24,16},{9,1},{17,9},{25,17},{10,2},{18,10},{26,18},{... | collective-permute-start | bytes 3932168 | tf_op jit(solution)/shard_map/ppermute | solution.py:26
  163.0 23.7 %all-to-all-done.3 = f32[8,2,5,2,16,128]{5,4,3,2,1,0:T(8,128)S(1)} async-done(((f32[8,2,5,2,16,128]{5,4,3,2,1,0:T(8,128)}), f32[8,2,5,2,16,128]{5,4,3,2,1,0:T(8,128)S(1)}, u32[]{:S(2)}, u32[]{:S(2)}) %all-to-all-start.3) | async-done | bytes 1310752 | tf_op jit(solution)/shard_map/all_to_all | solution.py:142
  189.8 4.7 %collective-permute-start.5 = (f32[2,5,2,128,128]{4,3,2,1,0:T(8,128)S(1)}, f32[2,5,2,128,128]{4,3,2,1,0:T(8,128)}, u32[]{:S(2)}, u32[]{:S(2)}) collective-permute-start(f32[2,5,2,128,128]{4,3,2,1,0:T(8,128)S(1)} %convolution_add_fusion.refs_2_), channel_id=1, source_target_pairs={{0,8},{8,16},{16,24},{1,9},{9,17},{17,25},{2,10},{10,18},{18,26},{... | collective-permute-start | bytes 3932168 | tf_op jit(solution)/shard_map/ppermute | solution.py:26
  194.5 2.1 fusion.14
  196.5 2.6 %pad_maximum_fusion.20 = f32[4]{0:T(128)S(1)} fusion(f32[1]{0:T(128)} %bitcast.86, f32[1]{0:T(128)} %bitcast.85, f32[1]{0:T(128)} %bitcast.84, f32[1]{0:T(128)} %bitcast.45), kind=kLoop, calls=%fused_computation.324 | loop fusion | flops 12 | bytes 32 | tf_op jit(solution)/shard_map/stack | solution.py:160
  199.7 2.6 %all-to-all-start.4 = ((f32[32,1,4]{2,1,0:T(1,128)}), f32[32,1,4]{2,1,0:T(1,128)S(1)}, u32[]{:S(2)}, u32[]{:S(2)}) async-start(f32[32,1,4]{2,1,0:T(1,128)} %broadcast_in_dim.99), calls=%async_computation.4 | async-start | bytes 32768 | tf_op jit(solution)/shard_map/all_to_all | solution.py:161
  202.4 6.9 %all-to-all-done.4 = f32[32,1,4]{2,1,0:T(1,128)S(1)} async-done(((f32[32,1,4]{2,1,0:T(1,128)}), f32[32,1,4]{2,1,0:T(1,128)S(1)}, u32[]{:S(2)}, u32[]{:S(2)}) %all-to-all-start.4) | async-done | bytes 544 | tf_op jit(solution)/shard_map/all_to_all | solution.py:161
  211.2 7.3 %mix.1 = f32[4,5,2,128,128]{4,3,2,1,0:T(8,128)} custom-call(f32[4,8]{1,0:T(4,128)S(1)} %select_add_fusion.matrix, f32[2,5,2,128,128]{4,3,2,1,0:T(8,128)} %collective-permute-done.5.refs_0_, f32[2,5,2,128,128]{4,3,2,1,0:T(8,128)S(1)} %convolution_add_fusion.1.refs_1_, f32[2,5,2,128,128]{4,3,2,1,0:T(8,128)S(1)} %convolution_add_fusion.refs_2_, ...), custom_call_target="tpu_custom_call" | custom-call | flops 6553600 | bytes 7864320 | tf_op jit(solution)/shard_map/mix/pallas_call | solution.py:190
  (112 shorter events, 32.4 us)
Async XLA Ops:
  0.0 2.6 %copy-start = (f32[4,5,2,128,128]{4,3,2,1,0:T(8,128)S(1)}, f32[4,5,2,128,128]{4,3,2,1,0:T(8,128)}, u32[]{:S(2)}) copy-start(f32[4,5,2,128,128]{4,3,2,1,0:T(8,128)} %param.3) | copy-start | bytes 7864324
  2.7 36.2 %collective-permute-start = (f32[2,4,1,128,128]{4,3,0,2,1:T(8,128)S(1)}, f32[2,4,1,128,128]{4,3,0,2,1:T(8,128)S(1)}, u32[]{:S(2)}, u32[]{:S(2)}) collective-permute-start(f32[2,4,1,128,128]{4,3,0,2,1:T(8,128)S(1)} %pad_maximum_fusion), channel_id=1, source_target_pairs={{0,7},{1,0},{2,1},{3,2},{4,3},{5,4},{6,5},{7,6},{8,15},{9,8},{10,9... | collective-permute-start | bytes 1572872 | tf_op jit(solution)/shard_map/ppermute | solution.py:26
  7.9 31.9 %collective-permute-start.1 = (f32[2,4,1,128,128]{4,3,0,2,1:T(8,128)S(1)}, f32[2,4,1,128,128]{4,3,0,2,1:T(8,128)S(1)}, u32[]{:S(2)}, u32[]{:S(2)}) collective-permute-start(f32[2,4,1,128,128]{4,3,0,2,1:T(8,128)S(1)} %pad_maximum_fusion.1), channel_id=1, source_target_pairs={{0,1},{1,2},{2,3},{3,4},{4,5},{5,6},{6,7},{7,0},{8,9},{9,10},{10,1... | collective-permute-start | bytes 1572872 | tf_op jit(solution)/shard_map/ppermute | solution.py:26
  8.8 42.2 %collective-permute-start.2 = (f32[2,4,1,128,128]{4,3,0,2,1:T(8,128)}, f32[2,4,1,128,128]{4,3,0,2,1:T(8,128)}, u32[]{:S(2)}, u32[]{:S(2)}) collective-permute-start(f32[2,4,1,128,128]{4,3,0,2,1:T(8,128)} %pad_maximum_fusion.2), channel_id=1, source_target_pairs={{0,7},{1,0},{2,1},{3,2},{4,3},{5,4},{6,5},{7,6},{8,15},{9,8},{10,9... | collective-permute-start | bytes 1572872 | tf_op jit(solution)/shard_map/ppermute | solution.py:26
  13.8 38.6 %collective-permute-start.3 = (f32[2,4,1,128,128]{4,3,0,2,1:T(8,128)}, f32[2,4,1,128,128]{4,3,0,2,1:T(8,128)}, u32[]{:S(2)}, u32[]{:S(2)}) collective-permute-start(f32[2,4,1,128,128]{4,3,0,2,1:T(8,128)} %pad_maximum_fusion.3), channel_id=1, source_target_pairs={{0,1},{1,2},{2,3},{3,4},{4,5},{5,6},{6,7},{7,0},{8,9},{9,10},{10,1... | collective-permute-start | bytes 1572872 | tf_op jit(solution)/shard_map/ppermute | solution.py:26
  46.1 33.8 %all-to-all-start = ((f32[8,2,5,2,16,128]{5,4,3,2,1,0:T(8,128)}), f32[8,2,5,2,16,128]{5,4,3,2,1,0:T(8,128)}, u32[]{:S(2)}, u32[]{:S(2)}) async-start(f32[8,2,5,2,16,128]{5,4,3,2,1,0:T(8,128)} %convolution_bitcast_fusion.4), calls=%async_computation | async-start | bytes 2621440 | tf_op jit(solution)/shard_map/all_to_all | solution.py:139
  52.3 1.3 copy-start.10
  52.3 1.3 copy-start.11
  55.1 1.0 copy-start.6
  55.1 1.0 copy-start.7
  55.1 1.1 copy-start.8
  55.1 1.2 copy-start.9
  56.7 1.0 copy-start.4
  56.7 1.0 copy-start.5
  80.0 35.9 %all-to-all-start.2 = ((f32[8,2,5,2,16,128]{5,4,3,2,1,0:T(8,128)}), f32[8,2,5,2,16,128]{5,4,3,2,1,0:T(8,128)S(1)}, u32[]{:S(2)}, u32[]{:S(2)}) async-start(f32[8,2,5,2,16,128]{5,4,3,2,1,0:T(8,128)} %convolution_bitcast_fusion.1), calls=%async_computation.2 | async-start | bytes 2621440 | tf_op jit(solution)/shard_map/all_to_all | solution.py:139
  115.9 34.8 %all-to-all-start.1 = ((f32[8,2,5,2,16,128]{5,4,3,2,1,0:T(8,128)}), f32[8,2,5,2,16,128]{5,4,3,2,1,0:T(8,128)}, u32[]{:S(2)}, u32[]{:S(2)}) async-start(f32[8,2,5,2,16,128]{5,4,3,2,1,0:T(8,128)} %copy.92), calls=%async_computation.1 | async-start | bytes 2621440 | tf_op jit(solution)/shard_map/all_to_all | solution.py:142
  150.7 36.0 %all-to-all-start.3 = ((f32[8,2,5,2,16,128]{5,4,3,2,1,0:T(8,128)}), f32[8,2,5,2,16,128]{5,4,3,2,1,0:T(8,128)S(1)}, u32[]{:S(2)}, u32[]{:S(2)}) async-start(f32[8,2,5,2,16,128]{5,4,3,2,1,0:T(8,128)} %copy.116), calls=%async_computation.3 | async-start | bytes 2621440 | tf_op jit(solution)/shard_map/all_to_all | solution.py:142
  156.0 2.8 %copy-start.1 = (f32[4,5,2,128,128]{4,3,2,1,0:T(8,128)S(1)}, f32[4,5,2,128,128]{4,3,2,1,0:T(8,128)}, u32[]{:S(2)}) copy-start(f32[4,5,2,128,128]{4,3,2,1,0:T(8,128)} %param.3) | copy-start | bytes 7864324
  160.2 34.3 %collective-permute-start.4 = (f32[2,5,2,128,128]{4,3,2,1,0:T(8,128)S(1)}, f32[2,5,2,128,128]{4,3,2,1,0:T(8,128)}, u32[]{:S(2)}, u32[]{:S(2)}) collective-permute-start(f32[2,5,2,128,128]{4,3,2,1,0:T(8,128)S(1)} %convolution_add_fusion.1.refs_1_), channel_id=1, source_target_pairs={{8,0},{16,8},{24,16},{9,1},{17,9},{25,17},{10,2},{18,10},{26,18},{... | collective-permute-start | bytes 3932168 | tf_op jit(solution)/shard_map/ppermute | solution.py:26
  186.7 1.7 copy-start.2
  189.8 12.6 %copy-start.12 = (s32[4]{0:T(128)S(1)}, s32[4]{0:T(128)}, u32[]{:S(2)}) copy-start(s32[4]{0:T(128)} %param.4) | copy-start | bytes 52
  189.8 20.7 %copy-start.13 = (f32[4]{0:T(128)S(1)}, f32[4]{0:T(128)}, u32[]{:S(2)}) copy-start(f32[4]{0:T(128)} %param.5) | copy-start | bytes 52
  189.8 21.4 %collective-permute-start.5 = (f32[2,5,2,128,128]{4,3,2,1,0:T(8,128)S(1)}, f32[2,5,2,128,128]{4,3,2,1,0:T(8,128)}, u32[]{:S(2)}, u32[]{:S(2)}) collective-permute-start(f32[2,5,2,128,128]{4,3,2,1,0:T(8,128)S(1)} %convolution_add_fusion.refs_2_), channel_id=1, source_target_pairs={{0,8},{8,16},{16,24},{1,9},{9,17},{17,25},{2,10},{10,18},{18,26},{... | collective-permute-start | bytes 3932168 | tf_op jit(solution)/shard_map/ppermute | solution.py:26
  199.7 9.5 %all-to-all-start.4 = ((f32[32,1,4]{2,1,0:T(1,128)}), f32[32,1,4]{2,1,0:T(1,128)S(1)}, u32[]{:S(2)}, u32[]{:S(2)}) async-start(f32[32,1,4]{2,1,0:T(1,128)} %broadcast_in_dim.99), calls=%async_computation.4 | async-start | bytes 32768 | tf_op jit(solution)/shard_map/all_to_all | solution.py:161
  (1 other events, 0.9 us)
